TPU v7x, 256 devices: a whole 4x4x8 slice. The times are simulated.
256 devices in a mesh: rows: 8 (over x, core), wide: 32 (over z, y).
Axes of the slice: x: 4, y: 4, z: 8, core: 2. Of those that a mesh axis runs over, the one named last changes fastest.
Arguments:
- inverse_first: float32 [2, 512, 512], P(None, 'rows'), may hold values from -1.5 to 1.5, as said below
- inverse_second: float32 [2, 512, 512], P(None, 'rows'), may hold values from -1.5 to 1.5, as said below
- coupling: float32 [2, 512, 512], P(None, None, 'rows'), may hold values from -0.1875 to 0.1875
- head_rhs: float32 [2, 1024, 1024], P(None, None, 'wide'), may hold values from -6 to 6
- panel_rows: bfloat16 [131072, 2048], P(('rows', 'wide')), may hold values from -0.125 to 0.125
- trail_rhs: float32 [2, 131072, 1024], P(None, ('rows', 'wide')), may hold values from -6 to 6
Outputs:
- solved_first: float32 [2, 512, 1024], P(None, 'rows', 'wide')
- solved_second: float32 [2, 512, 1024], P(None, 'rows', 'wide')
- trail_updated: float32 [2, 131072, 1024], P(None, ('rows', 'wide'))
Inputs may be any that keep to these rules, and one draw needn't show every extreme that they name: `inverse_first`: lower triangular in both planes: every entry above the diagonal is zero. `inverse_second`: lower triangular in both planes: every entry above the diagonal is zero.
All inputs are finite; a program needn't handle non-finite values.
Results may differ from a plain program's by a relative error of at most 0.0025.
Values may be sent and summed in bfloat16 or wider, within the bound.
A program may use at most 64 MiB of HBM per device.

v0:
```python
import jax
import jax.numpy as jnp
from jax import lax
from jax.sharding import PartitionSpec as P


def carried_in(part, axis, combine, identity):
    place = lax.axis_index(axis)
    gathered = lax.all_gather(part, axis)
    state = jnp.zeros_like(part) + jnp.asarray(identity, part.dtype)

    def one(hop, state):
        return combine(state, lax.dynamic_index_in_dim(gathered, hop, 0, False))

    return lax.fori_loop(0, place, one, state)


def spread(block, axis, holder):
    block = jnp.where(lax.axis_index(axis) == holder, block, jnp.zeros_like(block))
    return lax.psum(block, axis)


def complex_mul(left, right):
    highest = lax.Precision.HIGHEST
    real_part = jnp.dot(
        left[0], right[0], precision=highest, preferred_element_type=jnp.float32
    ) - jnp.dot(left[1], right[1], precision=highest, preferred_element_type=jnp.float32)
    imag_part = jnp.dot(
        left[0], right[1], precision=highest, preferred_element_type=jnp.float32
    ) + jnp.dot(left[1], right[0], precision=highest, preferred_element_type=jnp.float32)
    return jnp.stack([real_part, imag_part])


def add_terms(earlier, later):
    return earlier + later


def body(inverse_first, inverse_second, coupling, head_rhs, panel_rows, trail_rhs):
    block_size = coupling.shape[1]
    window = 2 * block_size
    solved_first = complex_mul(inverse_first, head_rhs[:, :block_size])
    partial_value = complex_mul(coupling, solved_first)
    before = carried_in(partial_value, "rows", add_terms, jnp.zeros_like(partial_value))
    summed = spread(before + partial_value, "rows", lax.axis_size("rows") - 1)
    solved_second = complex_mul(inverse_second, head_rhs[:, block_size:] - summed)
    solved_low = jnp.stack([solved_first, solved_second], 1).astype(jnp.bfloat16)
    solved_whole = lax.all_gather(solved_low, "rows", axis=2, tiled=True)
    contract = (((0,), (1,)), ((), ()))
    piece = lax.all_gather(solved_whole, "wide", axis=3, tiled=True)
    columns = piece.shape[3]
    real_low = piece[0].reshape(window, columns)
    imag_low = piece[1].reshape(window, columns)
    stack_real = jnp.concatenate([real_low, -imag_low], 0)
    stack_imag = jnp.concatenate([imag_low, real_low], 0)
    real_part = lax.dot_general(
        stack_real, panel_rows, contract, preferred_element_type=jnp.float32
    )
    imag_part = lax.dot_general(
        stack_imag, panel_rows, contract, preferred_element_type=jnp.float32
    )
    products = jnp.stack([real_part, imag_part])
    trail_updated = trail_rhs - jnp.transpose(products, (0, 2, 1))
    return (solved_first, solved_second, trail_updated)


def solution(mesh):
    return jax.shard_map(
        body,
        mesh=mesh,
        in_specs=(
            P(None, "rows", None),
            P(None, "rows", None),
            P(None, None, "rows"),
            P(None, None, "wide"),
            P(("rows", "wide"), None),
            P(None, ("rows", "wide"), None),
        ),
        out_specs=(
            P(None, "rows", "wide"),
            P(None, "rows", "wide"),
            P(None, ("rows", "wide"), None),
        ),
        check_vma=False,
    )
```

profile of v0, /device:TPU:1, one launch (start us, length us, event | category | flops | bytes accessed | tf_op | source)
XLA Modules:
  0.0 261.9 jit_solution(15770127748107482159)
XLA Ops:
  7.2 0.0 copy-start
  7.2 0.0 all-gather.6.cloned.1.call-start
  7.2 1.3 fusion.33
  8.5 1.1 fusion.35
  9.7 1.1 convolution_add_fusion.2
  10.8 1.1 convolution_subtract_fusion.2
  12.0 0.0 copy-start.7
  12.0 1.1 fusion.29
  13.1 1.1 fusion.27
  14.2 1.1 fusion.16
  15.3 0.0 copy-done.7
  15.3 0.0 copy-start.5
  15.3 1.1 fusion.15
  16.4 0.0 copy-done.5
  16.4 0.0 copy-start.6
  16.5 0.6 copy-done.6
  17.1 0.7 pad_maximum_fusion
  17.7 0.0 all-gather.6.cloned.1.call-update
  17.8 0.0 all-reduce.2.cloned.1.call-start
  17.8 30.2 %all-gather.6.cloned.1.call-done = f32[16,512,32]{1,2,0:T(8,128)} async-done(((f32[2,512,32]{1,2,0:T(8,128)}), f32[16,512,32]{1,2,0:T(8,128)}) %all-gather.6.cloned.1.call-update) | async-done | bytes 1048592 | tf_op jit(solution)/shard_map/all_gather | solution.py:9
  48.1 0.0 copy-start.4
  48.1 1.3 while.10
  48.1 1.0 constant_dynamic-slice_fusion.2
  49.1 0.2 copy.41
  49.3 0.1 bitcast_add_fusion.2
  49.4 0.2 copy.30
  49.6 1.6 add_select_fusion
  51.1 0.0 all-reduce.2.cloned.1.call-update
  51.1 0.0 all-gather.4.cloned.1.call-start
  51.2 1.3 convert_bitcast_fusion.1
  52.5 67.3 %all-reduce.2.cloned.1.call-done = f32[2,512,32]{1,2,0:T(8,128)} async-done(((f32[2,512,32]{1,2,0:T(8,128)}), f32[2,512,32]{1,2,0:T(8,128)}) %all-reduce.2.cloned.1.call-update) | async-done | bytes 131088 | tf_op jit(solution)/shard_map/psum | solution.py:20
  119.8 1.0 slice_subtract_fusion
  120.8 0.0 copy-done.4
  120.8 0.2 fusion.21
  121.1 0.2 fusion.23
  121.3 0.2 fusion.17
  121.6 0.2 fusion.18
  121.8 0.6 convert_bitcast_fusion
  122.4 0.1 copy.31
  122.6 15.7 %all_gather.14 = bf16[2,2,512,32]{3,1,0,2:T(2,128)(2,1)S(1)} all-gather(bf16[2,2,64,32]{3,1,0,2:T(2,128)(2,1)S(1)} %copy.31), channel_id=1, replica_groups=mesh['rows'=8,'wide'=32] {'rows'}, dimensions={2}, use_global_device_ids=true | all-gather | bytes 147456 | tf_op jit(solution)/shard_map/all_gather | solution.py:47
  138.3 1.3 copy.32
  139.6 0.0 all-gather.4.cloned.1.call-update
  139.6 5.4 %copy.35 = f32[2,512,1024]{1,2,0:T(8,128)} copy(f32[2,512,1024]{2,1,0:T(8,128)} %param.13) | data formatting | bytes 8388608 | tf_op args[5]
  145.0 73.3 %all-gather.4.cloned.1.call-done = bf16[2,2,512,1024]{2,1,0,3:T(2,128)(2,1)} async-done(((bf16[2,2,512,32]{2,1,0,3:T(2,128)(2,1)}), bf16[2,2,512,1024]{2,1,0,3:T(2,128)(2,1)}) %all-gather.4.cloned.1.call-update) | async-done | bytes 4194320 | tf_op jit(solution)/shard_map/all_gather | solution.py:49
  218.3 6.1 %fusion.59 = (bf16[1,2,512,1024]{2,1,0,3:T(2,128)(2,1)}, bf16[1,2,512,1024]{2,1,0,3:T(2,128)(2,1)}) fusion(bf16[2,2,512,1024]{2,1,0,3:T(2,128)(2,1)} %all-gather.4.cloned.1.call-done), kind=kLoop, calls=%fused_computation.75 | loop fusion | bytes 8388608 | tf_op jit(solution)/shard_map/slice | solution.py:52
  224.3 6.2 %copy.39 = bf16[1,2,512,1024]{3,2,1,0:T(8,128)(2,1)} copy(bf16[1,2,512,1024]{2,1,0,3:T(2,128)(2,1)} %get-tuple-element.67) | data formatting | bytes 4194304
  230.6 3.1 %bitcast_negate_fusion = bf16[1024,1024]{1,0:T(8,128)(2,1)} fusion(bf16[1,2,512,1024]{3,2,1,0:T(8,128)(2,1)} %copy.39), kind=kLoop, calls=%fused_computation.74 | loop fusion | flops 1048576 | bytes 4194304 | tf_op jit(solution)/shard_map/neg | solution.py:53
  233.6 6.2 %copy.38 = bf16[1,2,512,1024]{3,2,1,0:T(8,128)(2,1)} copy(bf16[1,2,512,1024]{2,1,0,3:T(2,128)(2,1)} %get-tuple-element.68) | data formatting | bytes 4194304
  239.8 0.0 copy-done
  239.8 0.0 copy-start.2
  239.8 0.0 copy-start.3
  239.8 4.8 %fusion.9 = f32[1,1024,512]{2,1,0:T(8,128)S(1)} fusion(bf16[512,2048]{1,0:T(8,128)(2,1)S(1)} %copy-done, bf16[1024,1024]{1,0:T(8,128)(2,1)} %bitcast.93, bf16[1024,1024]{1,0:T(8,128)(2,1)} %bitcast.92), kind=kOutput, calls=%fused_computation.12 | convolution fusion | flops 2155872256 | bytes 8388608 | tf_op jit(solution)/shard_map/dot_general | solution.py:58
  244.6 0.0 copy-done.2
  244.6 0.0 copy-done.3
  244.6 0.0 copy-start.1
  244.6 2.4 fusion.12
  247.0 0.0 copy-done.1
  247.0 3.0 %fusion.8 = f32[2,512,1024]{1,2,0:T(8,128)} fusion(f32[2,512,1024]{1,2,0:T(8,128)S(1)} %copy-done.1, f32[1,1024,512]{2,1,0:T(8,128)S(1)} %fusion.9, f32[1,1024,512]{2,1,0:T(8,128)S(1)} %fusion.12), kind=kLoop, calls=%fused_computation.11 | loop fusion | flops 2097152 | bytes 12582912 | tf_op jit(solution)/shard_map/sub | solution.py:62
  250.0 5.3 %copy.36 = f32[2,512,1024]{2,1,0:T(8,128)} copy(f32[2,512,1024]{1,2,0:T(8,128)} %fusion.8) | data formatting | bytes 8388608
  (2 shorter events, 0.0 us)
Async XLA Ops:
  7.2 232.7 %copy-start = (bf16[512,2048]{1,0:T(8,128)(2,1)S(1)}, bf16[512,2048]{1,0:T(8,128)(2,1)}, u32[]{:S(2)}) copy-start(bf16[512,2048]{1,0:T(8,128)(2,1)} %param.12) | copy-start | bytes 6291460
  7.2 40.9 %all-gather.6.cloned.1.call-start = ((), (), s32[]{:S(2)}) async-start(), calls=%async_computation.2 | async-start | bytes 1179648 | tf_op jit(solution)/shard_map/all_gather | solution.py:9
  12.0 3.3 %copy-start.7 = (f32[64,32]{0,1:T(8,128)}, f32[64,32]{0,1:T(8,128)S(1)}, u32[]{:S(2)}) copy-start(f32[64,32]{0,1:T(8,128)S(1)} %convolution_subtract_fusion.2) | copy-start | bytes 24580
  15.3 1.1 copy-start.5
  16.4 0.6 copy-start.6
  17.8 102.1 %all-reduce.2.cloned.1.call-start = ((), (), s32[]{:S(2)}) async-start(), calls=%async_computation | async-start | bytes 262144 | tf_op jit(solution)/shard_map/psum | solution.py:20
  48.1 72.8 %copy-start.4 = (f32[2,64,512]{2,1,0:T(8,128)S(1)}, f32[2,64,512]{2,1,0:T(8,128)}, u32[]{:S(2)}) copy-start(f32[2,64,512]{2,1,0:T(8,128)} %param.9) | copy-start | bytes 786436
  51.1 167.1 %all-gather.4.cloned.1.call-start = ((), (), s32[]{:S(2)}) async-start(), calls=%async_computation.1 | async-start | bytes 4325376 | tf_op jit(solution)/shard_map/all_gather | solution.py:49
  239.8 4.8 %copy-start.2 = (bf16[1024,1024]{1,0:T(8,128)(2,1)S(1)}, bf16[1024,1024]{1,0:T(8,128)(2,1)}, u32[]{:S(2)}) copy-start(bf16[1024,1024]{1,0:T(8,128)(2,1)} %bitcast_negate_fusion) | copy-start | bytes 6291460
  239.8 4.8 %copy-start.3 = (bf16[1,2,512,1024]{3,2,1,0:T(8,128)(2,1)S(1)}, bf16[1,2,512,1024]{3,2,1,0:T(8,128)(2,1)}, u32[]{:S(2)}) copy-start(bf16[1,2,512,1024]{3,2,1,0:T(8,128)(2,1)} %copy.38) | copy-start | bytes 6291460
  244.6 2.4 copy-start.1
Sparse Core Ops, SparseCore 0:
  17.9 30.1 all-gather.5
  51.3 68.5 all-reduce.1
  139.7 78.4 all-gather.3
where the time goes:
time: 265 us; the launch traced here: 262 us
  waiting for transfers between devices  171 us (65%)
  local copies, waits for them, and re-layouts  32.6 us (12%)
  matrix products  17.2 us (6%)
  blocking collectives  15.7 us (6%)
  between operations  14 us (5%)
  other arithmetic  11.3 us (4%)
    all_gather x1, waiting for transfers between devices, body(): piece = lax.all_gather(solved_whole, 'wide', axis=3, tiled=True)  73.3 us
    psum x1, waiting for transfers between devices, spread(): return lax.psum(block, axis)  67.3 us
    all_gather x1, waiting for transfers between devices, carried_in(): gathered = lax.all_gather(part, axis)  30.2 us
    unnamed x20, local copies, waits for them, and re-layouts  23.8 us
    all_gather x1, blocking collectives, body(): solved_whole = lax.all_gather(solved_low, 'rows', axis=2, tiled=True)  15.7 us
    slice x1, local copies, waits for them, and re-layouts, body(): imag_low = piece[1].reshape(window, columns)  6.08 us
  transfers between devices with their start and end apart: 3, of which 3 were waited for; matrix products, arithmetic and copies ran while one was open for 3% of the time, Pallas kernels for 0%

commit v1 on v0

v1 whole, which is shorter than its diff:
```python
import functools

import jax
import jax.numpy as jnp
from jax import lax
from jax.experimental import pallas as pl
from jax.experimental.pallas import tpu as pltpu
from jax.sharding import PartitionSpec as P

MESH = pl.DeviceIdType.MESH
F32 = jnp.float32
BF16 = jnp.bfloat16
NX, NY, NZ = 4, 4, 8
NT = (((1,), (1,)), ((), ()))
NN = (((1,), (0,)), ((), ()))


def split(value):
    high = value.astype(BF16)
    return high, (value - high.astype(F32)).astype(BF16)


def dot3(left, right, dims):
    left_high, left_low = split(left)
    right_high, right_low = split(right)
    dot = functools.partial(lax.dot_general, dimension_numbers=dims, preferred_element_type=F32)
    return dot(left_high, right_high) + (dot(left_low, right_high) + dot(left_high, right_low))


def swap(value):
    return pltpu.roll(value, 64, 1)


def first_lanes(shape):
    return lax.broadcasted_iota(jnp.int32, shape, 1) < 64


def solve(rhs, inverse):
    both = dot3(rhs, inverse, NT)
    top, low = both[:32], swap(both[32:])
    return jnp.where(first_lanes(top.shape), top - low, top + low)


class Net:
    def __init__(self, gathered, sems):
        self.g = gathered
        self.sems = sems
        self.rows = lax.axis_index("rows")
        self.wide = lax.axis_index("wide")
        self.x, self.core = lax.div(self.rows, 2), lax.rem(self.rows, 2)
        self.z, self.y = lax.div(self.wide, NY), lax.rem(self.wide, NY)

    def at_x(self, step):
        return lax.rem(self.x + (step + NX), NX)

    def at_y(self, step):
        return lax.rem(self.y + (step + NY), NY)

    def at_z(self, step):
        return lax.rem(self.z + (step + NZ), NZ)

    def copy(self, ref, kind, half, index, rows, wide):
        send, recv = self.sems[kind]
        return pltpu.make_async_remote_copy(
            src_ref=ref,
            dst_ref=ref,
            send_sem=send.at[half, index],
            recv_sem=recv.at[half, index],
            device_id=(rows, wide),
            device_id_type=MESH,
        )

    def own(self):
        return self.z, pl.ds(pl.multiple_of(self.y * 32, 32), 32)

    def sibling(self):
        return self.rows + 1 - 2 * self.core

    def to_sibling(self, ref, half, index):
        return self.copy(ref, "sib", half, index, self.sibling(), self.wide)


class Even(Net):
    def first(self, half, back=False):
        z, cols = self.own()
        out = []
        for j in range(1, NX):
            at = self.at_x(-j) if back else self.x
            ref = self.g.at[half, 0, at, z, cols]
            out.append(self.copy(ref, "one", half, j, 2 * self.at_x(j), self.wide))
        return out

    def second(self, half, back=False):
        out = []
        for j in range(1, NY):
            y = self.at_y(-j) if back else self.y
            ref = self.g.at[half, 0, :, self.z, pl.ds(pl.multiple_of(y * 32, 32), 32)]
            out.append(self.copy(ref, "two", half, j, self.rows, self.z * NY + self.at_y(j)))
        return out

    def ring(self, half, way, step, chunk, back=False):
        z = self.at_z(-way * (step if back else step - 1))
        ref = self.g.at[half, 0, pl.ds(2 * chunk, 2), z]
        index = (0 if way == 1 else 8) + (step - 1) * 2 + chunk
        return self.copy(ref, "ring", half, index, self.rows, self.at_z(way) * NY + self.y)

    def hops(self, step):
        if step == 4:
            return [(1, 0), (-1, 1)]
        return [(1, 0), (-1, 1), (1, 1), (-1, 0)]

    steps = 4

    def sib(self, half, step):
        moves = {0: [(0, 0)], 4: [(4, 4)]}.get(step, [(step, -step), (step + 4, step)])
        return [
            self.to_sibling(self.g.at[half, 0, :, self.at_z(move)], half, index)
            for index, move in moves
        ]


class Odd(Net):
    def first(self, half, back=False):
        cols = self.own()[1]
        out = []
        for j in range(1, NZ):
            z = self.at_z(-j) if back else self.z
            ref = self.g.at[half, 1, self.x, z, cols]
            out.append(self.copy(ref, "one", half, j, self.rows, self.at_z(j) * NY + self.y))
        return out

    def second(self, half, back=False):
        out = []
        for j in range(1, NY):
            y = self.at_y(-j) if back else self.y
            ref = self.g.at[half, 1, self.x, :, pl.ds(pl.multiple_of(y * 32, 32), 32)]
            out.append(self.copy(ref, "two", half, j, self.rows, self.z * NY + self.at_y(j)))
        return out

    def ring(self, half, way, step, chunk, back=False):
        x = self.at_x(-way * (step if back else step - 1))
        ref = self.g.at[half, 1, x, pl.ds(2 * chunk, 2)]
        index = (0 if way == 1 else 8) + (step - 1) * 4 + chunk
        return self.copy(ref, "ring", half, index, 2 * self.at_x(way) + 1, self.wide)

    def hops(self, step):
        if step == 2:
            return [(1, 0), (-1, 2), (1, 1), (-1, 3)]
        return [(1, 0), (-1, 2), (1, 1), (-1, 3), (1, 2), (-1, 0), (1, 3), (-1, 1)]

    steps = 2

    def sib(self, half, step):
        moves = {0: [(0, 0)], 1: [(1, -1), (2, 1)], 2: [(3, 2)]}[step]
        return [
            self.to_sibling(self.g.at[half, 1, self.at_x(move)], half, index)
            for index, move in moves
        ]


def kernel(
    inv1_hbm, inv2_hbm, coup_hbm, head_hbm, panel_hbm, trail_hbm,
    out1, out2, acc,
    inv1, inv2, coup, head, panel, lhs, gathered, parts, sums, whole,
    local, rs_send, rs_recv, ag_send, ag_recv,
    one_send, one_recv, two_send, two_recv, ring_send, ring_recv, sib_send, sib_recv,
):
    loads = [
        pltpu.make_async_copy(src, dst, local.at[i])
        for i, (src, dst) in enumerate(
            [
                (head_hbm, head),
                (inv1_hbm, inv1),
                (coup_hbm, coup),
                (inv2_hbm, inv2),
                (panel_hbm, panel),
                (trail_hbm, acc),
            ]
        )
    ]
    for load in loads:
        load.start()

    sems = {
        "one": (one_send, one_recv),
        "two": (two_send, two_recv),
        "ring": (ring_send, ring_recv),
        "sib": (sib_send, sib_recv),
    }
    nets = Even(gathered, sems), Odd(gathered, sems)
    me = nets[0]
    rows, wide, x, core = me.rows, me.wide, me.x, me.core

    def by_core(step):
        for at, net in enumerate(nets):
            pl.when(core == at)(functools.partial(step, net))

    barrier = pltpu.get_barrier_semaphore()

    def greet(rows_at, wide_at):
        pl.semaphore_signal(barrier, inc=1, device_id=(rows_at, wide_at), device_id_type=MESH)

    def enter(net):
        for j in range(1, 2 * NX):
            greet(lax.rem(rows + j, 2 * NX), wide)
        for j in range(1, NY):
            greet(rows, me.z * NY + me.at_y(j))
        z_steps = (1, -1) if net is nets[0] else range(1, NZ)
        for j in z_steps:
            greet(rows, me.at_z(j) * NY + me.y)

    by_core(enter)

    loads[0].wait()
    loads[1].wait()
    solved = solve(head[:, :512], inv1[...])
    own_z, own_cols = me.own()
    gathered[0, core, x, own_z, own_cols, :] = solved.astype(BF16)
    first = first_lanes(solved.shape)
    turned = swap(solved)
    out1[0] = solved[:, :64]
    out1[1] = turned[:, :64]
    loads[2].wait()
    left = jnp.concatenate([jnp.where(first, solved, -solved), turned], 0)
    parts[...] = dot3(left, coup[...], NN).reshape(parts.shape)

    by_core(
        lambda net: pl.semaphore_wait(barrier, 2 * NX - 1 + NY - 1 + (2 if net is nets[0] else NZ - 1))
    )

    def peer(j):
        return lax.rem(rows + j, 2 * NX)

    def reduce_copy(j):
        return pltpu.make_async_remote_copy(
            src_ref=parts.at[peer(j)],
            dst_ref=sums.at[j],
            send_sem=rs_send.at[j],
            recv_sem=rs_recv.at[j],
            device_id=(peer(j), wide),
            device_id_type=MESH,
        )

    def share_copy(j, back=False):
        ref = whole.at[peer(2 * NX - j) if back else rows]
        return pltpu.make_async_remote_copy(
            src_ref=ref,
            dst_ref=ref,
            send_sem=ag_send.at[j],
            recv_sem=ag_recv.at[j],
            device_id=(peer(j), wide),
            device_id_type=MESH,
        )

    def start(copies):
        for copy in copies:
            copy.start()

    def arrive(copies):
        for copy in copies:
            copy.wait_recv()

    order = (4, 3, 5, 2, 6, 1, 7)
    for j in order:
        reduce_copy(j).start()
    by_core(lambda net: start(net.first(0)))

    loads[4].wait()
    for half in range(2):
        for at in range(NX):
            base = 512 * half + 128 * at
            real = panel[:, base : base + 128].astype(F32)
            imag = panel[:, 1024 + base : 1024 + base + 128].astype(F32)
            head_lanes = first_lanes(real.shape)
            real_turned, imag_turned = swap(real), swap(imag)
            for c in range(2):
                k = (4 * c + at) * 128
                if c == 0:
                    plane0 = jnp.where(head_lanes, -real, imag_turned)
                    plane1 = jnp.where(head_lanes, -imag, -real_turned)
                else:
                    plane0 = jnp.where(head_lanes, -real_turned, imag)
                    plane1 = jnp.where(head_lanes, -imag_turned, -real)
                lhs[half, 0, :, k : k + 128] = plane0.astype(BF16)
                lhs[half, 1, :, k : k + 128] = plane1.astype(BF16)

    for j in order:
        reduce_copy(j).wait_recv()
    total = parts[rows]
    for j in range(1, 2 * NX):
        total += sums[j]
    whole[rows] = head[pl.ds(pl.multiple_of(8 * rows, 8), 8), 512:] - total
    for j in order:
        share_copy(j).start()

    def step_two(net, half):
        arrive(net.first(half, back=True))
        start(net.second(half))

    def ring_open(net, half):
        arrive(net.second(half, back=True))
        start(net.ring(half, way, 1, chunk) for way, chunk in net.hops(1))
        start(net.sib(half, 0))

    def ring_step(net, half, step):
        following = net.hops(step + 1) if step < net.steps else []
        for way, chunk in net.hops(step):
            net.ring(half, way, step, chunk, back=True).wait_recv()
            if (way, chunk) in following:
                net.ring(half, way, step + 1, chunk).start()
        start(net.sib(half, step))

    def ring_rest(net, half):
        for step in range(1, net.steps + 1):
            ring_step(net, half, step)

    by_core(lambda net: step_two(net, 0))

    for j in order:
        share_copy(j, back=True).wait_recv()
    loads[3].wait()
    solved = solve(whole[...].reshape(64, 512), inv2[...])
    gathered[1, core, x, own_z, own_cols, :] = solved.astype(BF16)
    by_core(lambda net: start(net.first(1)))
    by_core(lambda net: ring_open(net, 0))
    out2[0] = solved[:, :64]
    out2[1] = swap(solved)[:, :64]
    by_core(lambda net: step_two(net, 1))
    by_core(lambda net: ring_step(net, 0, 1))
    by_core(lambda net: ring_open(net, 1))

    def rest(net):
        for step in range(2, net.steps + 1):
            ring_step(net, 0, step)
        ring_rest(net, 1)

    by_core(rest)

    def from_sibling(net, half):
        other = nets[1] if net is nets[0] else nets[0]
        for step in range(other.steps + 1):
            arrive(other.sib(half, step))

    by_core(lambda net: from_sibling(net, 0))
    by_core(lambda net: from_sibling(net, 1))
    loads[5].wait()

    def product(n, carry):
        cols = pl.ds(pl.multiple_of(n * 256, 256), 256)
        for plane in range(2):
            total = acc[plane, :, cols]
            for half in range(2):
                right = jnp.concatenate(
                    [
                        gathered[half, c, at, pl.ds(2 * n, 2)].reshape(256, 128)
                        for c in range(2)
                        for at in range(NX)
                    ],
                    1,
                )
                total += lax.dot_general(lhs[half, plane], right, NT, preferred_element_type=F32)
            acc[plane, :, cols] = total
        return carry

    lax.fori_loop(0, 4, product, 0)

    for j in order:
        reduce_copy(j).wait_send()
        share_copy(j).wait_send()

    def leave(net):
        for half in range(2):
            for copy in net.first(half) + net.second(half):
                copy.wait_send()
            for step in range(1, net.steps + 1):
                for way, chunk in net.hops(step):
                    net.ring(half, way, step, chunk).wait_send()
            for step in range(net.steps + 1):
                for copy in net.sib(half, step):
                    copy.wait_send()

    by_core(leave)


def body(inverse_first, inverse_second, coupling, head_rhs, panel_rows, trail_rhs):
    dma = pltpu.SemaphoreType.DMA
    first, second, updated = pl.pallas_call(
        kernel,
        out_shape=(
            pltpu.VMEM((2, 32, 64), F32),
            pltpu.VMEM((2, 32, 64), F32),
            pltpu.VMEM((2, 512, 1024), F32),
        ),
        in_specs=[pl.BlockSpec(memory_space=pl.ANY)] * 6,
        out_specs=[pl.BlockSpec(memory_space=pltpu.VMEM)] * 3,
        scratch_shapes=[
            pltpu.VMEM((128, 512), F32),
            pltpu.VMEM((128, 512), F32),
            pltpu.VMEM((128, 512), F32),
            pltpu.VMEM((64, 1024), F32),
            pltpu.VMEM((512, 2048), BF16),
            pltpu.VMEM((2, 2, 512, 1024), BF16),
            pltpu.VMEM((2, 2, NX, NZ, 128, 128), BF16),
            pltpu.VMEM((8, 8, 512), F32),
            pltpu.VMEM((8, 8, 512), F32),
            pltpu.VMEM((8, 8, 512), F32),
            dma((6,)),
            dma((8,)),
            dma((8,)),
            dma((8,)),
            dma((8,)),
            dma((2, 8)),
            dma((2, 8)),
            dma((2, 4)),
            dma((2, 4)),
            dma((2, 16)),
            dma((2, 16)),
            dma((2, 8)),
            dma((2, 8)),
        ],
        compiler_params=pltpu.CompilerParams(
            collective_id=0, has_side_effects=True, vmem_limit_bytes=40 << 20
        ),
        cost_estimate=pl.CostEstimate(flops=4 << 30, bytes_accessed=12 << 20, transcendentals=0),
    )(
        inverse_first.reshape(128, 512),
        inverse_second.reshape(128, 512),
        jnp.transpose(coupling, (0, 2, 1)).reshape(128, 512),
        jnp.transpose(head_rhs, (0, 2, 1)).reshape(64, 1024),
        panel_rows,
        trail_rhs,
    )
    return jnp.transpose(first, (0, 2, 1)), jnp.transpose(second, (0, 2, 1)), updated


def solution(mesh):
    return jax.shard_map(
        body,
        mesh=mesh,
        in_specs=(
            P(None, "rows", None),
            P(None, "rows", None),
            P(None, None, "rows"),
            P(None, None, "wide"),
            P(("rows", "wide"), None),
            P(None, ("rows", "wide"), None),
        ),
        out_specs=(
            P(None, "rows", "wide"),
            P(None, "rows", "wide"),
            P(None, ("rows", "wide"), None),
        ),
        check_vma=False,
    )
```

time: 265 us -> 65.9 us (0.25); the launches traced: 262 us -> 65.6 us
  waiting for transfers between devices: 171 us -> 0 us
  Pallas kernels: 0 us -> 54.2 us
  local copies, waits for them, and re-layouts: 32.6 us -> 10.8 us
  matrix products: 17.2 us -> 0 us
  blocking collectives: 15.7 us -> 0 us
  between operations: 14 us -> 0.65 us
  other arithmetic: 11.3 us -> 0 us
    all_gather x2 -> x0, waiting for transfers between devices: 103 us -> none  [the longest x1 73.3 us: body(): piece = lax.all_gather(solved_whole, 'wide', axis=3, tiled=True)]
    psum x1 -> x0, waiting for transfers between devices: 67.3 us -> none  [spread(): return lax.psum(block, axis)]
    pallas_call x0 -> x1, Pallas kernels: none -> 54.2 us  [body(): pl.pallas_call(kernel, out_shape=(pltpu.VMEM((2, 32, 64), F32), pltpu.VME...]
    dot_general x14 -> x0, matrix products: 17.2 us -> none  [the longest x1 4.75 us: body(): lax.dot_general(stack_imag, panel_rows, contract, preferred_element_type=...]
    all_gather x1 -> x0, blocking collectives: 15.7 us -> none  [body(): solved_whole = lax.all_gather(solved_low, 'rows', axis=2, tiled=True)]
    unnamed x20 -> x15, local copies, waits for them, and re-layouts: 23.8 us -> 10.8 us
    slice x1 -> x0, local copies, waits for them, and re-layouts: 6.08 us -> none  [body(): imag_low = piece[1].reshape(window, columns)]
    sub x2 -> x0, other arithmetic: 3.96 us -> none  [the longest x1 2.98 us: body(): trail_updated = trail_rhs - jnp.transpose(products, (0, 2, 1))]
  transfers between devices with their start and end apart: 3 -> 0, of which waited for: 3 -> 0; matrix products, arithmetic and copies ran while one was open for 3% -> 0% of each run, Pallas kernels for 0% -> 0%
where the time goes in v1:
time: 65.9 us; the launch traced here: 65.6 us
  Pallas kernels  54.2 us (82%)
  local copies, waits for them, and re-layouts  10.8 us (16%)
    pallas_call x1, Pallas kernels, body(): pl.pallas_call(kernel, out_shape=(pltpu.VMEM((2, 32, 64), F32), pltpu.VME...  54.2 us
    unnamed x15, local copies, waits for them, and re-layouts  10.8 us

profile of v1, /device:TPU:1, one launch (start us, length us, event | category | flops | bytes accessed | tf_op | source)
XLA Modules:
  0.0 65.6 jit_solution(1007210087054626390)
XLA Ops:
  0.6 0.0 copy-start
  0.6 2.2 %copy-done = f32[2,512,1024]{2,1,0:T(8,128)S(1)} copy-done((f32[2,512,1024]{2,1,0:T(8,128)S(1)}, f32[2,512,1024]{2,1,0:T(8,128)}, u32[]{:S(2)}) %copy-start) | copy-done | bytes 4194328
  2.8 0.0 copy-start.1
  2.8 1.6 %copy-done.1 = bf16[512,2048]{1,0:T(8,128)(2,1)S(1)} copy-done((bf16[512,2048]{1,0:T(8,128)(2,1)S(1)}, bf16[512,2048]{1,0:T(8,128)(2,1)}, u32[]{:S(2)}) %copy-start.1) | copy-done | bytes 2097176
  4.4 0.0 copy-start.2
  4.4 0.9 %copy-done.2 = f32[2,64,512]{2,1,0:T(8,128)S(1)} copy-done((f32[2,64,512]{2,1,0:T(8,128)S(1)}, f32[2,64,512]{2,1,0:T(8,128)}, u32[]{:S(2)}) %copy-start.2) | copy-done | bytes 262168
  5.4 0.0 copy-start.3
  5.4 0.9 %copy-done.3 = f32[2,64,512]{2,1,0:T(8,128)S(1)} copy-done((f32[2,64,512]{2,1,0:T(8,128)S(1)}, f32[2,64,512]{2,1,0:T(8,128)}, u32[]{:S(2)}) %copy-start.3) | copy-done | bytes 262168
  6.3 0.0 copy-start.4
  6.3 0.9 %copy-done.4 = f32[2,512,64]{1,2,0:T(8,128)S(1)} copy-done((f32[2,512,64]{1,2,0:T(8,128)S(1)}, f32[2,512,64]{1,2,0:T(8,128)}, u32[]{:S(2)}) %copy-start.4) | copy-done | bytes 262168
  7.3 0.0 copy-start.5
  7.3 0.9 %copy-done.5 = f32[2,1024,32]{1,2,0:T(8,128)S(1)} copy-done((f32[2,1024,32]{1,2,0:T(8,128)S(1)}, f32[2,1024,32]{1,2,0:T(8,128)}, u32[]{:S(2)}) %copy-start.5) | copy-done | bytes 262168
  8.2 54.2 %shard_map.85 = (f32[2,32,64]{2,1,0:T(8,128)S(1)}, f32[2,32,64]{2,1,0:T(8,128)S(1)}, f32[2,512,1024]{2,1,0:T(8,128)S(1)}) custom-call(f32[128,512]{1,0:T(8,128)S(1)} %bitcast.12, f32[128,512]{1,0:T(8,128)S(1)} %bitcast.13, f32[128,512]{1,0:T(8,128)S(1)} %bitcast.14, f32[64,1024]{1,0:T(8,128)S(1)} %bitcast.15, bf16[512,2048]{1,0:T(8,128)(2,1)S(1)} %copy-done.1, ...), custom_call_target="tpu_custom_call" | custom-call | flops 4294967296 | bytes 12582912 | tf_op jit(solution)/shard_map/pallas_call | solution.py:387
  62.4 0.6 copy.12
  63.0 0.6 copy.13
  63.6 2.0 %copy.14 = f32[2,512,1024]{2,1,0:T(8,128)} copy(f32[2,512,1024]{2,1,0:T(8,128)S(1)} %get-tuple-element.11) | data formatting | bytes 8388608
Async XLA Ops:
  0.6 2.2 %copy-start = (f32[2,512,1024]{2,1,0:T(8,128)S(1)}, f32[2,512,1024]{2,1,0:T(8,128)}, u32[]{:S(2)}) copy-start(f32[2,512,1024]{2,1,0:T(8,128)} %trail_hbm.1) | copy-start | bytes 12582916
  2.8 1.6 %copy-start.1 = (bf16[512,2048]{1,0:T(8,128)(2,1)S(1)}, bf16[512,2048]{1,0:T(8,128)(2,1)}, u32[]{:S(2)}) copy-start(bf16[512,2048]{1,0:T(8,128)(2,1)} %panel_hbm.1) | copy-start | bytes 6291460
  4.4 0.9 %copy-start.2 = (f32[2,64,512]{2,1,0:T(8,128)S(1)}, f32[2,64,512]{2,1,0:T(8,128)}, u32[]{:S(2)}) copy-start(f32[2,64,512]{2,1,0:T(8,128)} %param.6) | copy-start | bytes 786436
  5.4 0.9 %copy-start.3 = (f32[2,64,512]{2,1,0:T(8,128)S(1)}, f32[2,64,512]{2,1,0:T(8,128)}, u32[]{:S(2)}) copy-start(f32[2,64,512]{2,1,0:T(8,128)} %param.7) | copy-start | bytes 786436
  6.3 0.9 %copy-start.4 = (f32[2,512,64]{1,2,0:T(8,128)S(1)}, f32[2,512,64]{1,2,0:T(8,128)}, u32[]{:S(2)}) copy-start(f32[2,512,64]{1,2,0:T(8,128)} %param.8) | copy-start | bytes 786436
  7.3 0.9 %copy-start.5 = (f32[2,1024,32]{1,2,0:T(8,128)S(1)}, f32[2,1024,32]{1,2,0:T(8,128)}, u32[]{:S(2)}) copy-start(f32[2,1024,32]{1,2,0:T(8,128)} %param.9) | copy-start | bytes 786436

commit v2 on v0

v2 whole, which is shorter than its diff:
```python
import functools

import jax
import jax.numpy as jnp
from jax import lax
from jax.experimental import pallas as pl
from jax.experimental.pallas import tpu as pltpu
from jax.sharding import PartitionSpec as P

MESH = pl.DeviceIdType.MESH
F32 = jnp.float32
BF16 = jnp.bfloat16
NX, NY, NZ = 4, 4, 8
NEAR = ((2, 2), (2, 1))
PLANE = sorted(
    ((i, j) for i in range(NX) for j in range(NY) if i or j),
    key=lambda p: -(min(p[0], NX - p[0]) + min(p[1], NY - p[1])),
)
NT = (((1,), (1,)), ((), ()))
NN = (((1,), (0,)), ((), ()))


def split(value):
    high = value.astype(BF16)
    return high, (value - high.astype(F32)).astype(BF16)


def dot3(left, right, dims):
    left_high, left_low = split(left)
    right_high, right_low = split(right)
    dot = functools.partial(lax.dot_general, dimension_numbers=dims, preferred_element_type=F32)
    return dot(left_high, right_high) + (dot(left_low, right_high) + dot(left_high, right_low))


def swap(value):
    return pltpu.roll(value, 64, 1)


def first_lanes(shape):
    return lax.broadcasted_iota(jnp.int32, shape, 1) < 64


def solve(rhs, inverse):
    both = dot3(rhs, inverse, NT)
    top, low = both[:32], swap(both[32:])
    return jnp.where(first_lanes(top.shape), top - low, top + low)


class Net:
    def __init__(self, gathered, sems):
        self.g, self.sems = gathered, sems
        self.rows, self.wide = lax.axis_index("rows"), lax.axis_index("wide")
        self.x, self.core = lax.div(self.rows, 2), lax.rem(self.rows, 2)
        self.z, self.y = lax.div(self.wide, NY), lax.rem(self.wide, NY)

    def on_rows(self, j):
        return lax.rem(self.rows + j, 2 * NX), self.wide

    def on_plane(self, i, j):
        x, y = lax.rem(self.x + i, NX), lax.rem(self.y + j, NY)
        return 2 * x + self.core, self.z * NY + y

    def on_z(self, j):
        return self.rows, lax.rem(self.z + j, NZ) * NY + self.y

    def sibling(self):
        return self.rows + 1 - 2 * self.core, self.wide

    def copy(self, src, dst, kind, half, index, to):
        send, recv = self.sems[kind]
        return pltpu.make_async_remote_copy(
            src_ref=src,
            dst_ref=dst,
            send_sem=send.at[half, index],
            recv_sem=recv.at[half, index],
            device_id=to,
            device_id_type=MESH,
        )

    def block(self, half, dz, i=0, j=0, core=None):
        x, y = lax.rem(self.x + (NX - i), NX), lax.rem(self.y + (NY - j), NY)
        return self.g.at[half, self.core if core is None else core, dz, y, x]

    def slab(self, half, dz, core=None):
        return self.g.at[half, self.core if core is None else core, dz]

    def far(self, half, near, i=0, j=0, core=None):
        return self.block(half, pl.ds(near + 1, NZ - 1 - 2 * near), i, j, core)

    def along_z(self, half, j):
        return self.copy(self.block(half, 0), self.block(half, NZ - j), "z", half, j, self.on_z(j))

    def over_plane(self, half, i, j, back=False):
        ref = self.block(half, 0, i, j) if back else self.block(half, 0)
        return self.copy(ref, ref, "p", half, NY * i + j, self.on_plane(i, j))

    def slab_along_z(self, half, j):
        return self.copy(self.slab(half, 0), self.slab(half, NZ - j), "b", half, j, self.on_z(j))

    def far_over(self, half, near, i, j, back=False):
        ref = self.far(half, near, i, j) if back else self.far(half, near)
        return self.copy(ref, ref, "f", half, NY * i + j, self.on_plane(i, j))

    def pass_slab(self, half, dz, back=False):
        ref = self.slab(half, dz, 1 - self.core if back else None)
        return self.copy(ref, ref, "s", half, 16 + dz, self.sibling())

    def pass_far(self, half, near, i, j, back=False):
        ref = self.far(half, near, i, j, 1 - self.core if back else None)
        return self.copy(ref, ref, "s", half, NY * i + j, self.sibling())


    def open(self, half, near):
        for j in far_steps(near):
            self.along_z(half, j).start()
        for i, j in PLANE:
            self.over_plane(half, i, j).start()

    def spread_plane(self, half, near):
        for i, j in PLANE[::-1]:
            self.over_plane(half, i, j, back=True).wait_recv()
        for j in near_steps(near):
            self.slab_along_z(half, j).start()
        self.pass_slab(half, 0).start()

    def spread_z(self, half, near):
        for j in far_steps(near)[::-1]:
            self.along_z(half, j).wait_recv()
        for i, j in PLANE:
            self.far_over(half, near, i, j).start()
        self.pass_far(half, near, 0, 0).start()

    def take_slabs(self, half, near):
        for j in near_steps(near):
            self.slab_along_z(half, j).wait_recv()
            self.pass_slab(half, NZ - j).start()

    def take_far(self, half, near):
        for i, j in PLANE[::-1]:
            self.far_over(half, near, i, j, back=True).wait_recv()
            self.pass_far(half, near, i, j).start()

    def finish(self, half, near):
        for dz in [0] + near_steps(near):
            self.pass_slab(half, dz, back=True).wait_recv()
        for i, j in [(0, 0)] + PLANE[::-1]:
            self.pass_far(half, near, i, j, back=True).wait_recv()

    def leave(self, half, near):
        for j in far_steps(near):
            self.along_z(half, j).wait_send()
        for i, j in PLANE:
            self.over_plane(half, i, j).wait_send()
            self.far_over(half, near, i, j).wait_send()
            self.pass_far(half, near, i, j).wait_send()
        self.pass_far(half, near, 0, 0).wait_send()
        for j in near_steps(near):
            self.slab_along_z(half, j).wait_send()
        for dz in [0] + near_steps(near):
            self.pass_slab(half, dz).wait_send()


def far_steps(near):
    return sorted(range(near + 1, NZ - near), key=lambda j: -min(j, NZ - j))


def near_steps(near):
    return [j for step in range(1, near + 1) for j in (step, NZ - step)]


def update(acc, lhs, gathered, half, plane, steps, columns):
    right = jnp.concatenate(
        [
            jnp.concatenate([gathered[half, c, dz, :, x].reshape(128, 128) for dz in steps], 0)
            for c in range(2)
            for x in range(NX)
        ],
        1,
    )
    product = lax.dot_general(lhs[half, plane], right, NT, preferred_element_type=F32)
    return [
        acc[plane, :, cols] + product[:, 128 * at : 128 * (at + 1)]
        for at, cols in enumerate(columns)
    ]


def columns_of(z, steps):
    return [pl.ds(pl.multiple_of(128 * lax.rem(z + dz, NZ), 128), 128) for dz in steps]


PAIRS = ((0, 1), (7, 2), (6, 3), (5, 4))


def gather_kernel(
    inv1_hbm, inv2_hbm, coup_hbm, head_hbm, panel_hbm, trail_hbm,
    out1, out2, acc, lhs, gathered,
    inv1, inv2, coup, head, panel, parts, sums, whole,
    local, rs_send, rs_recv, ag_send, ag_recv,
    z_send, z_recv, p_send, p_recv, b_send, b_recv, f_send, f_recv, s_send, s_recv,
):
    loads = [
        pltpu.make_async_copy(src, dst, local.at[i])
        for i, (src, dst) in enumerate(
            [
                (head_hbm, head),
                (inv1_hbm, inv1),
                (coup_hbm, coup),
                (inv2_hbm, inv2),
                (panel_hbm, panel),
                (trail_hbm, acc),
            ]
        )
    ]
    for load in loads:
        load.start()

    net = Net(
        gathered,
        {
            "z": (z_send, z_recv),
            "p": (p_send, p_recv),
            "b": (b_send, b_recv),
            "f": (f_send, f_recv),
            "s": (s_send, s_recv),
        },
    )
    rows, x, core = net.rows, net.x, net.core

    def stage(step, half, other=False):
        near = NEAR[half][::-1] if other else NEAR[half]
        if near[0] == near[1]:
            step(half, near[0])
        else:
            for at in range(2):
                pl.when(core == at)(functools.partial(step, half, near[at]))

    barrier = pltpu.get_barrier_semaphore()
    peers = [net.on_z(j) for j in far_steps(0)]
    peers += [net.on_plane(i, j) for i, j in PLANE if j]
    peers += [net.on_rows(j) for j in range(1, 2 * NX)]
    for peer in peers:
        pl.semaphore_signal(barrier, inc=1, device_id=peer, device_id_type=MESH)

    loads[0].wait()
    loads[1].wait()
    solved = solve(head[:, :512], inv1[...])
    gathered[0, core, 0, net.y, x] = solved.astype(BF16)
    first = first_lanes(solved.shape)
    turned = swap(solved)
    out1[0] = solved[:, :64]
    out1[1] = turned[:, :64]
    loads[2].wait()
    left = jnp.concatenate([jnp.where(first, solved, -solved), turned], 0)
    parts[...] = dot3(left, coup[...], NN).reshape(parts.shape)

    pl.semaphore_wait(barrier, len(peers))

    def reduce_copy(j):
        to = net.on_rows(j)
        return pltpu.make_async_remote_copy(
            src_ref=parts.at[to[0]],
            dst_ref=sums.at[j],
            send_sem=rs_send.at[j],
            recv_sem=rs_recv.at[j],
            device_id=to,
            device_id_type=MESH,
        )

    def share_copy(j, back=False):
        ref = whole.at[lax.rem(rows + (2 * NX - j), 2 * NX) if back else rows]
        return pltpu.make_async_remote_copy(
            src_ref=ref,
            dst_ref=ref,
            send_sem=ag_send.at[j],
            recv_sem=ag_recv.at[j],
            device_id=net.on_rows(j),
            device_id_type=MESH,
        )

    order = (4, 3, 5, 2, 6, 1, 7)
    for j in order:
        reduce_copy(j).start()
    stage(net.open, 0)

    loads[4].wait()
    for half in range(2):
        for at in range(NX):
            base = 512 * half + 128 * at
            real = panel[:, base : base + 128].astype(F32)
            imag = panel[:, 1024 + base : 1024 + base + 128].astype(F32)
            head_lanes = first_lanes(real.shape)
            real_turned, imag_turned = swap(real), swap(imag)
            for c in range(2):
                k = (NX * c + at) * 128
                if c == 0:
                    plane0 = jnp.where(head_lanes, -real, imag_turned)
                    plane1 = jnp.where(head_lanes, -imag, -real_turned)
                else:
                    plane0 = jnp.where(head_lanes, -real_turned, imag)
                    plane1 = jnp.where(head_lanes, -imag_turned, -real)
                lhs[half, 0, :, k : k + 128] = plane0.astype(BF16)
                lhs[half, 1, :, k : k + 128] = plane1.astype(BF16)

    for j in order:
        reduce_copy(j).wait_recv()
    total = parts[rows]
    for j in range(1, 2 * NX):
        total += sums[j]
    whole[rows] = head[pl.ds(pl.multiple_of(8 * rows, 8), 8), 512:] - total
    for j in order:
        share_copy(j).start()

    stage(net.spread_plane, 0)
    for j in order:
        share_copy(j, back=True).wait_recv()
    loads[3].wait()
    solved = solve(whole[...].reshape(64, 512), inv2[...])
    gathered[1, core, 0, net.y, x] = solved.astype(BF16)
    stage(net.open, 1)
    out2[0] = solved[:, :64]
    out2[1] = swap(solved)[:, :64]

    stage(net.spread_z, 0)
    stage(net.take_slabs, 0)
    stage(net.spread_plane, 1)
    stage(net.spread_z, 1)
    stage(net.take_far, 0)
    stage(net.finish, 0, other=True)
    loads[5].wait()

    def product(at):
        columns = columns_of(net.z, PAIRS[at])
        for plane in range(2):
            for cols, value in zip(columns, update(acc, lhs, gathered, 0, plane, PAIRS[at], columns)):
                acc[plane, :, cols] = value

    product(0)
    product(1)
    stage(net.take_slabs, 1)
    product(2)
    product(3)
    stage(net.take_far, 1)
    stage(net.finish, 1, other=True)

    for j in order:
        reduce_copy(j).wait_send()
        share_copy(j).wait_send()
    stage(net.leave, 0)
    stage(net.leave, 1)


def write_kernel(first, second, acc, lhs, gathered, out1, out2, out, stage, sems):
    z = lax.div(lax.axis_index("wide"), NY)
    copies = [
        pltpu.make_async_copy(first, out1, sems.at[8]),
        pltpu.make_async_copy(second, out2, sems.at[9]),
    ]
    for copy in copies:
        copy.start()
    for at, steps in enumerate(PAIRS):
        columns = columns_of(z, steps)
        for plane in range(2):
            for cols, value in zip(columns, update(acc, lhs, gathered, 1, plane, steps, columns)):
                stage[plane, :, cols] = value
        for k, cols in enumerate(columns):
            copies.append(
                pltpu.make_async_copy(
                    stage.at[:, :, cols], out.at[:, :, cols], sems.at[2 * at + k]
                )
            )
            copies[-1].start()
    for copy in copies:
        copy.wait()


def body(inverse_first, inverse_second, coupling, head_rhs, panel_rows, trail_rhs):
    dma = pltpu.SemaphoreType.DMA
    pair = [dma((2, 16)), dma((2, 16))]
    held = pl.pallas_call(
        gather_kernel,
        out_shape=(
            pltpu.VMEM((2, 32, 64), F32),
            pltpu.VMEM((2, 32, 64), F32),
            pltpu.VMEM((2, 512, 1024), F32),
            pltpu.VMEM((2, 2, 512, 1024), BF16),
            pltpu.VMEM((2, 2, NZ, NY, NX, 32, 128), BF16),
        ),
        in_specs=[pl.BlockSpec(memory_space=pltpu.HBM)] * 6,
        out_specs=[pl.BlockSpec(memory_space=pltpu.VMEM)] * 5,
        scratch_shapes=[
            pltpu.VMEM((128, 512), F32),
            pltpu.VMEM((128, 512), F32),
            pltpu.VMEM((128, 512), F32),
            pltpu.VMEM((64, 1024), F32),
            pltpu.VMEM((512, 2048), BF16),
            pltpu.VMEM((8, 8, 512), F32),
            pltpu.VMEM((8, 8, 512), F32),
            pltpu.VMEM((8, 8, 512), F32),
            dma((6,)),
            dma((8,)),
            dma((8,)),
            dma((8,)),
            dma((8,)),
            *pair * 4,
            dma((2, 24)),
            dma((2, 24)),
        ],
        compiler_params=pltpu.CompilerParams(
            collective_id=0, has_side_effects=True, vmem_limit_bytes=24 << 20
        ),
        cost_estimate=pl.CostEstimate(flops=2 << 30, bytes_accessed=8 << 20, transcendentals=0),
    )(
        *(
            pltpu.with_memory_space_constraint(operand, pltpu.HBM)
            for operand in (
                inverse_first.reshape(128, 512),
                inverse_second.reshape(128, 512),
                jnp.transpose(coupling, (0, 2, 1)).reshape(128, 512),
                jnp.transpose(head_rhs, (0, 2, 1)).reshape(64, 1024),
                panel_rows,
                trail_rhs,
            )
        )
    )
    first, second, updated = pl.pallas_call(
        write_kernel,
        out_shape=(
            jax.ShapeDtypeStruct((2, 32, 64), F32),
            jax.ShapeDtypeStruct((2, 32, 64), F32),
            jax.ShapeDtypeStruct((2, 512, 1024), F32),
        ),
        in_specs=[pl.BlockSpec(memory_space=pltpu.VMEM)] * 5,
        out_specs=[pl.BlockSpec(memory_space=pltpu.HBM)] * 3,
        scratch_shapes=[pltpu.VMEM((2, 512, 1024), F32), dma((10,))],
        compiler_params=pltpu.CompilerParams(vmem_limit_bytes=16 << 20),
        cost_estimate=pl.CostEstimate(flops=2 << 30, bytes_accessed=4 << 20, transcendentals=0),
    )(*(pltpu.with_memory_space_constraint(value, pltpu.VMEM) for value in held))
    return jnp.transpose(first, (0, 2, 1)), jnp.transpose(second, (0, 2, 1)), updated


def solution(mesh):
    return jax.shard_map(
        body,
        mesh=mesh,
        in_specs=(
            P(None, "rows", None),
            P(None, "rows", None),
            P(None, None, "rows"),
            P(None, None, "wide"),
            P(("rows", "wide"), None),
            P(None, ("rows", "wide"), None),
        ),
        out_specs=(
            P(None, "rows", "wide"),
            P(None, "rows", "wide"),
            P(None, ("rows", "wide"), None),
        ),
        check_vma=False,
    )
```

time: 265 us -> 47 us (0.18); the launches traced: 262 us -> 46.9 us
  waiting for transfers between devices: 171 us -> 0 us
  Pallas kernels: 0 us -> 46.3 us
  local copies, waits for them, and re-layouts: 32.6 us -> 0 us
  matrix products: 17.2 us -> 0 us
  blocking collectives: 15.7 us -> 0 us
  between operations: 14 us -> 0.64 us
  other arithmetic: 11.3 us -> 0 us
    all_gather x2 -> x0, waiting for transfers between devices: 103 us -> none  [the longest x1 73.3 us: body(): piece = lax.all_gather(solved_whole, 'wide', axis=3, tiled=True)]
    psum x1 -> x0, waiting for transfers between devices: 67.3 us -> none  [spread(): return lax.psum(block, axis)]
    pallas_call x0 -> x2, Pallas kernels: none -> 46.3 us  [the longest x1 42 us: body(): pl.pallas_call(gather_kernel, out_shape=(pltpu.VMEM((2, 32, 64), F32), pl...]
    unnamed x20 -> x0, local copies, waits for them, and re-layouts: 23.8 us -> none
    dot_general x14 -> x0, matrix products: 17.2 us -> none  [the longest x1 4.75 us: body(): lax.dot_general(stack_imag, panel_rows, contract, preferred_element_type=...]
    all_gather x1 -> x0, blocking collectives: 15.7 us -> none  [body(): solved_whole = lax.all_gather(solved_low, 'rows', axis=2, tiled=True)]
    slice x1 -> x0, local copies, waits for them, and re-layouts: 6.08 us -> none  [body(): imag_low = piece[1].reshape(window, columns)]
    sub x2 -> x0, other arithmetic: 3.96 us -> none  [the longest x1 2.98 us: body(): trail_updated = trail_rhs - jnp.transpose(products, (0, 2, 1))]
  transfers between devices with their start and end apart: 3 -> 0, of which waited for: 3 -> 0; matrix products, arithmetic and copies ran while one was open for 3% -> 0% of each run, Pallas kernels for 0% -> 0%
where the time goes in v2:
time: 47 us; the launch traced here: 46.9 us
  Pallas kernels  46.3 us (99%)
  between operations  0.64 us (1%)
    pallas_call x1, Pallas kernels, body(): pl.pallas_call(gather_kernel, out_shape=(pltpu.VMEM((2, 32, 64), F32), pl...  42 us
    pallas_call x1, Pallas kernels, body(): pl.pallas_call(write_kernel, out_shape=(jax.ShapeDtypeStruct((2, 32, 64),...  4.33 us

profile of v2, /device:TPU:1, one launch (start us, length us, event | category | flops | bytes accessed | tf_op | source)
XLA Modules:
  0.0 46.9 jit_solution(18400638772835957085)
XLA Ops:
  0.6 42.0 %shard_map.85 = (f32[2,32,64]{2,1,0:T(8,128)S(1)}, f32[2,32,64]{2,1,0:T(8,128)S(1)}, f32[2,512,1024]{2,1,0:T(8,128)S(1)}, bf16[2,2,512,1024]{3,2,1,0:T(8,128)(2,1)S(1)}, bf16[2,2,8,4,4,32,128]{6,5,4,3,2,1,0:T(8,128)(2,1)S(1)}) custom-call(f32[128,512]{1,0:T(8,128)} %bitcast.10, f32[128,512]{1,0:T(8,128)} %bitcast.11, f32[128,512]{1,0:T(8,128)} %bitcast.12, ...), custom_call_target="tpu_custom_call" | custom-call | flops 2147483648 | bytes 8388608 | tf_op jit(solution)/shard_map/pallas_call | solution.py:379
  42.6 4.3 %shard_map.86 = (f32[2,32,64]{2,1,0:T(8,128)}, f32[2,32,64]{2,1,0:T(8,128)}, f32[2,512,1024]{2,1,0:T(8,128)}) custom-call(f32[2,32,64]{2,1,0:T(8,128)S(1)} %get-tuple-element.11.first, f32[2,32,64]{2,1,0:T(8,128)S(1)} %get-tuple-element.12.second, f32[2,512,1024]{2,1,0:T(8,128)S(1)} %get-tuple-element.13.acc, ...), custom_call_target="tpu_custom_call" | custom-call | flops 2147483648 | bytes 4194304 | tf_op jit(solution)/shard_map/pallas_call | solution.py:425

commit v3 on v2

v3 whole, which is shorter than its diff:
```python
import functools

import jax
import jax.numpy as jnp
from jax import lax
from jax.experimental import pallas as pl
from jax.experimental.pallas import tpu as pltpu
from jax.sharding import PartitionSpec as P

MESH = pl.DeviceIdType.MESH
F32 = jnp.float32
BF16 = jnp.bfloat16
NX, NY, NZ = 4, 4, 8
NEAR = ((2, 2), (2, 1))
RELAY = (0,)
PLANE = sorted(
    ((i, j) for i in range(NX) for j in range(NY) if i or j),
    key=lambda p: -(min(p[0], NX - p[0]) + min(p[1], NY - p[1])),
)
GROUPS, BOXES = (PLANE[-4:], PLANE[3:-4], PLANE[:3]), ((4, 1), (4, 2), (3, 1))
SENT_FIRST, SENT, SENT_ON = range(3)
OVER_PLANE, ALONG_Z, NEAR_ON, REST_ON, SLABS, FAR = 0, 1, 2, 3, 3, 6
NT = (((1,), (1,)), ((), ()))
NN = (((1,), (0,)), ((), ()))


def split(value):
    high = value.astype(BF16)
    return high, (value - high.astype(F32)).astype(BF16)


def dot3(left, right, dims):
    (left_high, left_low), (right_high, right_low) = left, right
    dot = functools.partial(lax.dot_general, dimension_numbers=dims, preferred_element_type=F32)
    return dot(left_high, right_high) + (dot(left_low, right_high) + dot(left_high, right_low))


def swap(value):
    return pltpu.roll(value, 64, 1)


def first_lanes(shape):
    return lax.broadcasted_iota(jnp.int32, shape, 1) < 64


def solve(rhs, inverse):
    both = dot3(split(rhs), inverse, NT)
    top, low = both[:32], swap(both[32:])
    return jnp.where(first_lanes(top.shape), top - low, top + low)


class Net:
    def __init__(self, gathered, sems):
        self.g, self.sems = gathered, sems
        self.rows, self.wide = lax.axis_index("rows"), lax.axis_index("wide")
        self.x, self.core = lax.div(self.rows, 2), lax.rem(self.rows, 2)
        self.z, self.y = lax.div(self.wide, NY), lax.rem(self.wide, NY)

    def on_rows(self, j):
        return lax.rem(self.rows + j, 2 * NX), self.wide

    def on_plane(self, i, j):
        x, y = lax.rem(self.x + i, NX), lax.rem(self.y + j, NY)
        return 2 * x + self.core, self.z * NY + y

    def on_z(self, j):
        return self.rows, lax.rem(self.z + j, NZ) * NY + self.y

    def sibling(self):
        return self.rows + 1 - 2 * self.core, self.wide

    def copy(self, src, dst, half, sent, landed, to):
        send, recv = self.sems
        return pltpu.make_async_remote_copy(
            src_ref=src,
            dst_ref=dst,
            send_sem=send.at[half, sent],
            recv_sem=recv.at[half, landed],
            device_id=to,
            device_id_type=MESH,
        )

    def block(self, half, dz, i=0, j=0, core=None):
        x, y = lax.rem(self.x + (NX - i), NX), lax.rem(self.y + (NY - j), NY)
        return self.g.at[half, self.core if core is None else core, dz, y, x]

    def slab(self, half, dz):
        return self.g.at[half, self.core, dz]

    def far(self, half, near):
        return self.block(half, pl.ds(near + 1, NZ - 1 - 2 * near))

    def along_z(self, half, j):
        src, dst = self.block(half, 0), self.block(half, NZ - j)
        return self.copy(src, dst, half, SENT, ALONG_Z, self.on_z(j))

    def over_plane(self, half, i, j):
        ref = self.block(half, 0)
        return self.copy(ref, ref, half, SENT_FIRST, OVER_PLANE, self.on_plane(i, j))

    def slabs_along_z(self, half, step):
        for j in (step, NZ - step):
            src, dst = self.slab(half, 0), self.slab(half, NZ - j)
            yield self.copy(src, dst, half, SENT, SLABS + step, self.on_z(j))

    def far_over(self, half, near, i, j):
        ref = self.far(half, near)
        landed = FAR + next(at for at, group in enumerate(GROUPS) if (i, j) in group)
        return self.copy(ref, ref, half, SENT, landed, self.on_plane(i, j))

    def hand_on(self, half, ref, landed):
        self.copy(ref, ref, half, SENT_ON, landed, self.sibling()).start()

    def wait(self, half, blocks, sent=None, landed=None):
        z, y, x = blocks
        ref = self.g.at[half, self.core, pl.ds(0, z), pl.ds(0, y), pl.ds(0, x)]
        copy = self.copy(ref, ref, half, sent or 0, landed or 0, self.sibling())
        if landed is None:
            copy.wait_send()
        else:
            copy.wait_recv()


    def open(self, half, near):
        for j in far_steps(near):
            self.along_z(half, j).start()
        for i, j in PLANE:
            self.over_plane(half, i, j).start()

    def spread_plane(self, half, near):
        self.wait(half, (5, 3, 1), landed=OVER_PLANE)
        for step in range(1, (1 if half in RELAY else near) + 1):
            for copy in self.slabs_along_z(half, step):
                copy.start()
        self.hand_on(half, self.slab(half, 0), NEAR_ON)

    def relay(self, half, near):
        self.wait(half, (2, NY, NX), landed=SLABS + 1)
        for dz, way in ((NZ - 1, 1), (1, NZ - 1)):
            src, dst = self.slab(half, dz), self.slab(half, 2 * dz % NZ)
            self.copy(src, dst, half, SENT, SLABS + 2, self.on_z(way)).start()
        for dz in (1, NZ - 1):
            self.hand_on(half, self.slab(half, dz), NEAR_ON)

    def spread_z(self, half, near):
        self.wait(half, (NZ - 1 - 2 * near, 1, 1), landed=ALONG_Z)
        for i, j in [(2, 2), (1, 2), (3, 2), (0, 2), (2, 1), (1, 1), (3, 1), (0, 1), (2, 3), (1, 3), (3, 3), (0, 3), (2, 0), (1, 0), (3, 0)]:
            self.far_over(half, near, i, j).start()
        self.hand_on(half, self.far(half, near), REST_ON)

    def take_slabs(self, half, near):
        for step in range(2 if half in RELAY else 1, near + 1):
            self.wait(half, (2, NY, NX), landed=SLABS + step)
            for dz in (step, NZ - step):
                self.hand_on(half, self.slab(half, dz), NEAR_ON if step == 1 else REST_ON)

    def take_far(self, half, near, at):
        count = NZ - 1 - 2 * near
        self.wait(half, (count, *BOXES[at]), landed=FAR + at)
        for i, j in GROUPS[at]:
            self.hand_on(half, self.block(half, pl.ds(near + 1, count), i, j), REST_ON)

    def finish_near(self, half):
        self.wait(half, (3, NY, NX), landed=NEAR_ON)

    def finish_rest(self, half):
        self.wait(half, (NZ - 3, NY, NX), landed=REST_ON)

    def leave(self, half):
        self.wait(half, (5, 3, 1), sent=SENT_FIRST)
        self.wait(half, (NZ - 1, NY, NX), sent=SENT)
        self.wait(half, (NZ, NY, NX), sent=SENT_ON)


def far_steps(near):
    return sorted(range(near + 1, NZ - near), key=lambda j: -min(j, NZ - j))


def update(acc, lhs, gathered, half, plane, steps, columns):
    right = jnp.concatenate(
        [
            jnp.concatenate([gathered[half, c, dz, :, x].reshape(128, 128) for dz in steps], 0)
            for c in range(2)
            for x in range(NX)
        ],
        1,
    )
    product = lax.dot_general(lhs[half, plane], right, NT, preferred_element_type=F32)
    return [
        acc[plane, :, cols] + product[:, 128 * at : 128 * (at + 1)]
        for at, cols in enumerate(columns)
    ]


def columns_of(z, steps):
    return [pl.ds(pl.multiple_of(128 * lax.rem(z + dz, NZ), 128), 128) for dz in steps]


NEAR_STEPS, REST_STEPS = ((0, 1), (7,)), ((2, 3), (4, 5), (6,))


def gather_kernel(
    inv1_hbm, inv2_hbm, coup_hbm, head_hbm, panel_hbm, trail_hbm,
    out1, out2, acc, lhs, gathered,
    inv1, inv2, coup, head, panel, parts, sums, whole, inv2_split,
    local, sum_sems, send_sems, recv_sems,
):
    loads = [
        pltpu.make_async_copy(src, dst, local.at[i])
        for i, (src, dst) in enumerate(
            [
                (head_hbm, head),
                (inv1_hbm, inv1),
                (coup_hbm, coup),
                (inv2_hbm, inv2),
                (panel_hbm, panel),
                (trail_hbm, acc),
            ]
        )
    ]
    for load in loads[:3]:
        load.start()

    net = Net(gathered, (send_sems, recv_sems))
    rows, x, core = net.rows, net.x, net.core

    def stage(step, half, *more):
        near = NEAR[half]
        if near[0] == near[1]:
            step(half, near[0], *more)
        else:
            for at in range(2):
                pl.when(core == at)(functools.partial(step, half, near[at], *more))

    barrier = pltpu.get_barrier_semaphore()
    peers = [net.on_z(j) for j in far_steps(0)]
    peers += [net.on_plane(i, j) for i, j in PLANE if j]
    peers += [net.on_rows(j) for j in range(1, 2 * NX)]
    for peer in peers:
        pl.semaphore_signal(barrier, inc=1, device_id=peer, device_id_type=MESH)

    loads[0].wait()
    loads[1].wait()
    for load in loads[3:]:
        load.start()
    solved = solve(head[:, :512], split(inv1[...]))
    gathered[0, core, 0, net.y, x] = solved.astype(BF16)
    first = first_lanes(solved.shape)
    turned = swap(solved)
    out1[0] = solved[:, :64]
    out1[1] = turned[:, :64]
    loads[2].wait()
    left = jnp.concatenate([jnp.where(first, solved, -solved), turned], 0)
    parts[...] = dot3(split(left), split(coup[...]), NN).reshape(parts.shape)

    pl.semaphore_wait(barrier, len(peers))

    def reduce_copy(j):
        to = net.on_rows(j)
        return pltpu.make_async_remote_copy(
            src_ref=parts.at[to[0]],
            dst_ref=sums.at[j],
            send_sem=sum_sems.at[0],
            recv_sem=sum_sems.at[1],
            device_id=to,
            device_id_type=MESH,
        )

    def share_copy(j):
        ref = whole.at[rows]
        return pltpu.make_async_remote_copy(
            src_ref=ref,
            dst_ref=ref,
            send_sem=sum_sems.at[2],
            recv_sem=sum_sems.at[3],
            device_id=net.on_rows(j),
            device_id_type=MESH,
        )

    def all_seven(ref, at):
        ref = ref.at[pl.ds(1, 2 * NX - 1)]
        return pltpu.make_async_remote_copy(
            src_ref=ref,
            dst_ref=ref,
            send_sem=sum_sems.at[at],
            recv_sem=sum_sems.at[at + 1],
            device_id=net.sibling(),
            device_id_type=MESH,
        )

    order = (4, 3, 5, 2, 6, 1, 7)
    for j in order:
        reduce_copy(j).start()
    stage(net.open, 0)

    loads[4].wait()
    for half in range(2):
        for at in range(NX):
            base = 512 * half + 128 * at
            real = panel[:, base : base + 128].astype(F32)
            imag = panel[:, 1024 + base : 1024 + base + 128].astype(F32)
            head_lanes = first_lanes(real.shape)
            real_turned, imag_turned = swap(real), swap(imag)
            for c in range(2):
                k = (NX * c + at) * 128
                if c == 0:
                    plane0 = jnp.where(head_lanes, -real, imag_turned)
                    plane1 = jnp.where(head_lanes, -imag, -real_turned)
                else:
                    plane0 = jnp.where(head_lanes, -real_turned, imag)
                    plane1 = jnp.where(head_lanes, -imag_turned, -real)
                lhs[half, 0, :, k : k + 128] = plane0.astype(BF16)
                lhs[half, 1, :, k : k + 128] = plane1.astype(BF16)

    loads[3].wait()
    inv2_split[0], inv2_split[1] = split(inv2[...])

    all_seven(sums, 0).wait_recv()
    total = parts[rows]
    for j in range(1, 2 * NX):
        total += sums[j]
    whole[rows] = head[pl.ds(pl.multiple_of(8 * rows, 8), 8), 512:] - total
    for j in order:
        share_copy(j).start()

    stage(net.spread_plane, 0)
    stage(net.spread_z, 0)
    all_seven(whole, 2).wait_recv()
    solved = solve(whole[...].reshape(64, 512), (inv2_split[0], inv2_split[1]))
    gathered[1, core, 0, net.y, x] = solved.astype(BF16)
    stage(net.open, 1)
    out2[0] = solved[:, :64]
    out2[1] = swap(solved)[:, :64]

    def product(half, steps):
        columns = columns_of(net.z, steps)
        for plane in range(2):
            for cols, value in zip(columns, update(acc, lhs, gathered, half, plane, steps, columns)):
                acc[plane, :, cols] = value

    stage(net.relay, 0)
    stage(net.spread_plane, 1)
    stage(net.spread_z, 1)
    stage(net.take_slabs, 0)
    stage(net.take_far, 0, 0)
    stage(net.take_far, 0, 1)
    stage(net.take_far, 0, 2)
    net.finish_near(0)
    loads[5].wait()
    product(0, (0, 1))
    net.finish_rest(0)
    product(0, (7, 2))
    product(0, (6, 3))
    product(0, (5, 4))
    stage(net.take_slabs, 1)
    stage(net.take_far, 1, 0)
    net.finish_near(1)
    product(1, (0, 1))
    stage(net.take_far, 1, 1)
    product(1, (7,))
    stage(net.take_far, 1, 2)
    net.finish_rest(1)
    all_seven(parts, 0).wait_send()
    all_seven(whole, 2).wait_send()
    net.leave(0)
    net.leave(1)


def write_kernel(first, second, acc, lhs, gathered, out1, out2, out, stage, sems):
    z = lax.div(lax.axis_index("wide"), NY)
    copies = [
        pltpu.make_async_copy(first, out1, sems.at[8]),
        pltpu.make_async_copy(second, out2, sems.at[9]),
    ]
    for copy in copies:
        copy.start()
    for steps in NEAR_STEPS:
        for dz, cols in zip(steps, columns_of(z, steps)):
            copies.append(
                pltpu.make_async_copy(acc.at[:, :, cols], out.at[:, :, cols], sems.at[dz])
            )
            copies[-1].start()
    for steps in REST_STEPS:
        columns = columns_of(z, steps)
        for plane in range(2):
            for cols, value in zip(columns, update(acc, lhs, gathered, 1, plane, steps, columns)):
                stage[plane, :, cols] = value
        for dz, cols in zip(steps, columns):
            copies.append(
                pltpu.make_async_copy(stage.at[:, :, cols], out.at[:, :, cols], sems.at[dz])
            )
            copies[-1].start()
    for copy in copies:
        copy.wait()


def body(inverse_first, inverse_second, coupling, head_rhs, panel_rows, trail_rhs):
    dma = pltpu.SemaphoreType.DMA
    held = pl.pallas_call(
        gather_kernel,
        out_shape=(
            pltpu.VMEM((2, 32, 64), F32),
            pltpu.VMEM((2, 32, 64), F32),
            pltpu.VMEM((2, 512, 1024), F32),
            pltpu.VMEM((2, 2, 512, 1024), BF16),
            pltpu.VMEM((2, 2, NZ, NY, NX, 32, 128), BF16),
        ),
        in_specs=[pl.BlockSpec(memory_space=pltpu.HBM)] * 6,
        out_specs=[pl.BlockSpec(memory_space=pltpu.VMEM)] * 5,
        scratch_shapes=[
            pltpu.VMEM((128, 512), F32),
            pltpu.VMEM((128, 512), F32),
            pltpu.VMEM((128, 512), F32),
            pltpu.VMEM((64, 1024), F32),
            pltpu.VMEM((512, 2048), BF16),
            pltpu.VMEM((8, 8, 512), F32),
            pltpu.VMEM((8, 8, 512), F32),
            pltpu.VMEM((8, 8, 512), F32),
            pltpu.VMEM((2, 128, 512), BF16),
            dma((6,)),
            dma((4,)),
            dma((2, 3)),
            dma((2, 9)),
        ],
        compiler_params=pltpu.CompilerParams(
            collective_id=0, has_side_effects=True, vmem_limit_bytes=24 << 20
        ),
        cost_estimate=pl.CostEstimate(flops=2 << 30, bytes_accessed=8 << 20, transcendentals=0),
    )(
        *(
            pltpu.with_memory_space_constraint(operand, pltpu.HBM)
            for operand in (
                inverse_first.reshape(128, 512),
                inverse_second.reshape(128, 512),
                jnp.transpose(coupling, (0, 2, 1)).reshape(128, 512),
                jnp.transpose(head_rhs, (0, 2, 1)).reshape(64, 1024),
                panel_rows,
                trail_rhs,
            )
        )
    )
    first, second, updated = pl.pallas_call(
        write_kernel,
        out_shape=(
            jax.ShapeDtypeStruct((2, 32, 64), F32),
            jax.ShapeDtypeStruct((2, 32, 64), F32),
            jax.ShapeDtypeStruct((2, 512, 1024), F32),
        ),
        in_specs=[pl.BlockSpec(memory_space=pltpu.VMEM)] * 5,
        out_specs=[pl.BlockSpec(memory_space=pltpu.HBM)] * 3,
        scratch_shapes=[pltpu.VMEM((2, 512, 1024), F32), dma((10,))],
        compiler_params=pltpu.CompilerParams(vmem_limit_bytes=16 << 20),
        cost_estimate=pl.CostEstimate(flops=2 << 30, bytes_accessed=4 << 20, transcendentals=0),
    )(*(pltpu.with_memory_space_constraint(value, pltpu.VMEM) for value in held))
    return jnp.transpose(first, (0, 2, 1)), jnp.transpose(second, (0, 2, 1)), updated


def solution(mesh):
    return jax.shard_map(
        body,
        mesh=mesh,
        in_specs=(
            P(None, "rows", None),
            P(None, "rows", None),
            P(None, None, "rows"),
            P(None, None, "wide"),
            P(("rows", "wide"), None),
            P(None, ("rows", "wide"), None),
        ),
        out_specs=(
            P(None, "rows", "wide"),
            P(None, "rows", "wide"),
            P(None, ("rows", "wide"), None),
        ),
        check_vma=False,
    )
```

time: 47 us -> 40.1 us (0.85)
  Pallas kernels: 46.3 us -> 39.3 us
    pallas_call x1, Pallas kernels: 42 us -> 36.1 us  [body(): pl.pallas_call(gather_kernel, out_shape=(pltpu.VMEM((2, 32, 64), F32), pl...]
    pallas_call x1, Pallas kernels: 4.33 us -> 3.19 us  [body(): pl.pallas_call(write_kernel, out_shape=(jax.ShapeDtypeStruct((2, 32, 64),...]
where the time goes in v3:
time: 40.1 us; the launch traced here: 40 us
  Pallas kernels  39.3 us (98%)
  between operations  0.64 us (2%)
    pallas_call x1, Pallas kernels, body(): pl.pallas_call(gather_kernel, out_shape=(pltpu.VMEM((2, 32, 64), F32), pl...  36.1 us
    pallas_call x1, Pallas kernels, body(): pl.pallas_call(write_kernel, out_shape=(jax.ShapeDtypeStruct((2, 32, 64),...  3.19 us

profile of v3, /device:TPU:1, one launch (start us, length us, event | category | flops | bytes accessed | tf_op | source)
XLA Modules:
  0.0 40.0 jit_solution(12130901525794658501)
XLA Ops:
  0.6 36.1 %shard_map.85 = (f32[2,32,64]{2,1,0:T(8,128)S(1)}, f32[2,32,64]{2,1,0:T(8,128)S(1)}, f32[2,512,1024]{2,1,0:T(8,128)S(1)}, bf16[2,2,512,1024]{3,2,1,0:T(8,128)(2,1)S(1)}, bf16[2,2,8,4,4,32,128]{6,5,4,3,2,1,0:T(8,128)(2,1)S(1)}) custom-call(f32[128,512]{1,0:T(8,128)} %bitcast.10, f32[128,512]{1,0:T(8,128)} %bitcast.11, f32[128,512]{1,0:T(8,128)} %bitcast.12, ...), custom_call_target="tpu_custom_call" | custom-call | flops 2147483648 | bytes 8388608 | tf_op jit(solution)/shard_map/pallas_call | solution.py:399
  36.8 3.2 %shard_map.86 = (f32[2,32,64]{2,1,0:T(8,128)}, f32[2,32,64]{2,1,0:T(8,128)}, f32[2,512,1024]{2,1,0:T(8,128)}) custom-call(f32[2,32,64]{2,1,0:T(8,128)S(1)} %get-tuple-element.11.first, f32[2,32,64]{2,1,0:T(8,128)S(1)} %get-tuple-element.12.second, f32[2,512,1024]{2,1,0:T(8,128)S(1)} %get-tuple-element.13.acc, ...), custom_call_target="tpu_custom_call" | custom-call | flops 2147483648 | bytes 4194304 | tf_op jit(solution)/shard_map/pallas_call | solution.py:442

commit v4 on v3

--- a/solution.py
+++ b/solution.py
@@ -17,9 +17,8 @@
     ((i, j) for i in range(NX) for j in range(NY) if i or j),
     key=lambda p: -(min(p[0], NX - p[0]) + min(p[1], NY - p[1])),
 )
-GROUPS, BOXES = (PLANE[-4:], PLANE[3:-4], PLANE[:3]), ((4, 1), (4, 2), (3, 1))
 SENT_FIRST, SENT, SENT_ON = range(3)
-OVER_PLANE, ALONG_Z, NEAR_ON, REST_ON, SLABS, FAR = 0, 1, 2, 3, 3, 6
+OVER_PLANE, ALONG_Z, SLABS, NEAR_ON, SLABS_ON, FAR, FAR_ON = 0, 1, 1, 4, 5, 6, 10
 NT = (((1,), (1,)), ((), ()))
 NN = (((1,), (0,)), ((), ()))
 
@@ -105,8 +104,7 @@
 
     def far_over(self, half, near, i, j):
         ref = self.far(half, near)
-        landed = FAR + next(at for at, group in enumerate(GROUPS) if (i, j) in group)
-        return self.copy(ref, ref, half, SENT, landed, self.on_plane(i, j))
+        return self.copy(ref, ref, half, SENT, FAR + i, self.on_plane(i, j))
 
     def hand_on(self, half, ref, landed):
         self.copy(ref, ref, half, SENT_ON, landed, self.sibling()).start()
@@ -146,25 +144,28 @@
         self.wait(half, (NZ - 1 - 2 * near, 1, 1), landed=ALONG_Z)
         for i, j in [(2, 2), (1, 2), (3, 2), (0, 2), (2, 1), (1, 1), (3, 1), (0, 1), (2, 3), (1, 3), (3, 3), (0, 3), (2, 0), (1, 0), (3, 0)]:
             self.far_over(half, near, i, j).start()
-        self.hand_on(half, self.far(half, near), REST_ON)
 
     def take_slabs(self, half, near):
         for step in range(2 if half in RELAY else 1, near + 1):
             self.wait(half, (2, NY, NX), landed=SLABS + step)
             for dz in (step, NZ - step):
-                self.hand_on(half, self.slab(half, dz), NEAR_ON if step == 1 else REST_ON)
-
-    def take_far(self, half, near, at):
+                self.hand_on(half, self.slab(half, dz), NEAR_ON if step == 1 else SLABS_ON)
+
+    def take_far(self, half, near, i):
         count = NZ - 1 - 2 * near
-        self.wait(half, (count, *BOXES[at]), landed=FAR + at)
-        for i, j in GROUPS[at]:
-            self.hand_on(half, self.block(half, pl.ds(near + 1, count), i, j), REST_ON)
+        self.wait(half, (count, NY - 1 if i == 0 else NY, 1), landed=FAR + i)
+        ref = self.g.at[half, self.core, pl.ds(near + 1, count), :, lax.rem(self.x + (NX - i), NX)]
+        self.hand_on(half, ref, FAR_ON + i)
 
     def finish_near(self, half):
         self.wait(half, (3, NY, NX), landed=NEAR_ON)
 
-    def finish_rest(self, half):
-        self.wait(half, (NZ - 3, NY, NX), landed=REST_ON)
+    def finish_slabs(self, half, near):
+        if near > 1:
+            self.wait(half, (2 * near - 2, NY, NX), landed=SLABS_ON)
+
+    def finish_far(self, half, near, i):
+        self.wait(half, (NZ - 1 - 2 * near, NY, 1), landed=FAR_ON + i)
 
     def leave(self, half):
         self.wait(half, (5, 3, 1), sent=SENT_FIRST)
@@ -176,20 +177,23 @@
     return sorted(range(near + 1, NZ - near), key=lambda j: -min(j, NZ - j))
 
 
-def update(acc, lhs, gathered, half, plane, steps, columns):
+def update(acc, out, lhs, gathered, half, steps, columns, core=None, planes=(0, 1)):
     right = jnp.concatenate(
         [
             jnp.concatenate([gathered[half, c, dz, :, x].reshape(128, 128) for dz in steps], 0)
-            for c in range(2)
+            for c in (range(2) if core is None else [core])
             for x in range(NX)
         ],
         1,
     )
-    product = lax.dot_general(lhs[half, plane], right, NT, preferred_element_type=F32)
-    return [
-        acc[plane, :, cols] + product[:, 128 * at : 128 * (at + 1)]
-        for at, cols in enumerate(columns)
-    ]
+    for plane in planes:
+        if core is None:
+            left = lhs[half, plane]
+        else:
+            left = lhs[half, plane, :, pl.ds(pl.multiple_of(128 * NX * core, 128 * NX), 128 * NX)]
+        product = lax.dot_general(left, right, NT, preferred_element_type=F32)
+        for at, cols in enumerate(columns):
+            out[plane, :, cols] = acc[plane, :, cols] + product[:, 128 * at : 128 * (at + 1)]
 
 
 def columns_of(z, steps):
@@ -224,8 +228,8 @@
     net = Net(gathered, (send_sems, recv_sems))
     rows, x, core = net.rows, net.x, net.core
 
-    def stage(step, half, *more):
-        near = NEAR[half]
+    def stage(step, half, *more, other=False):
+        near = NEAR[half][::-1] if other else NEAR[half]
         if near[0] == near[1]:
             step(half, near[0], *more)
         else:
@@ -332,11 +336,8 @@
     out2[0] = solved[:, :64]
     out2[1] = swap(solved)[:, :64]
 
-    def product(half, steps):
-        columns = columns_of(net.z, steps)
-        for plane in range(2):
-            for cols, value in zip(columns, update(acc, lhs, gathered, half, plane, steps, columns)):
-                acc[plane, :, cols] = value
+    def product(half, steps, *one):
+        update(acc, acc, lhs, gathered, half, steps, columns_of(net.z, steps), *one)
 
     stage(net.relay, 0)
     stage(net.spread_plane, 1)
@@ -344,22 +345,34 @@
     stage(net.take_slabs, 0)
     stage(net.take_far, 0, 0)
     stage(net.take_far, 0, 1)
+    stage(net.take_far, 0, 3)
     stage(net.take_far, 0, 2)
     net.finish_near(0)
     loads[5].wait()
     product(0, (0, 1))
-    net.finish_rest(0)
+    stage(net.finish_slabs, 0, other=True)
+    stage(net.finish_far, 0, 0, other=True)
+    stage(net.finish_far, 0, 1, other=True)
+    stage(net.finish_far, 0, 3, other=True)
+    stage(net.finish_far, 0, 2, other=True)
     product(0, (7, 2))
     product(0, (6, 3))
     product(0, (5, 4))
     stage(net.take_slabs, 1)
     stage(net.take_far, 1, 0)
+    stage(net.take_far, 1, 1)
+    stage(net.take_far, 1, 3)
+    stage(net.take_far, 1, 2)
     net.finish_near(1)
     product(1, (0, 1))
-    stage(net.take_far, 1, 1)
     product(1, (7,))
-    stage(net.take_far, 1, 2)
-    net.finish_rest(1)
+    for steps in REST_STEPS:
+        product(1, steps, core)
+    stage(net.finish_slabs, 1, other=True)
+    stage(net.finish_far, 1, 0, other=True)
+    stage(net.finish_far, 1, 1, other=True)
+    stage(net.finish_far, 1, 3, other=True)
+    stage(net.finish_far, 1, 2, other=True)
     all_seven(parts, 0).wait_send()
     all_seven(whole, 2).wait_send()
     net.leave(0)
@@ -367,7 +380,7 @@
 
 
 def write_kernel(first, second, acc, lhs, gathered, out1, out2, out, stage, sems):
-    z = lax.div(lax.axis_index("wide"), NY)
+    core, z = lax.rem(lax.axis_index("rows"), 2), lax.div(lax.axis_index("wide"), NY)
     copies = [
         pltpu.make_async_copy(first, out1, sems.at[8]),
         pltpu.make_async_copy(second, out2, sems.at[9]),
@@ -383,13 +396,12 @@
     for steps in REST_STEPS:
         columns = columns_of(z, steps)
         for plane in range(2):
-            for cols, value in zip(columns, update(acc, lhs, gathered, 1, plane, steps, columns)):
-                stage[plane, :, cols] = value
-        for dz, cols in zip(steps, columns):
-            copies.append(
-                pltpu.make_async_copy(stage.at[:, :, cols], out.at[:, :, cols], sems.at[dz])
-            )
-            copies[-1].start()
+            update(acc, stage, lhs, gathered, 1, steps, columns, 1 - core, (plane,))
+            for dz, cols in zip(steps, columns):
+                copies.append(
+                    pltpu.make_async_copy(stage.at[plane, :, cols], out.at[plane, :, cols], sems.at[10 + 8 * plane + dz])
+                )
+                copies[-1].start(priority=plane)
     for copy in copies:
         copy.wait()
 
@@ -420,7 +432,7 @@
             dma((6,)),
             dma((4,)),
             dma((2, 3)),
-            dma((2, 9)),
+            dma((2, 14)),
         ],
         compiler_params=pltpu.CompilerParams(
             collective_id=0, has_side_effects=True, vmem_limit_bytes=24 << 20
@@ -448,7 +460,7 @@
         ),
         in_specs=[pl.BlockSpec(memory_space=pltpu.VMEM)] * 5,
         out_specs=[pl.BlockSpec(memory_space=pltpu.HBM)] * 3,
-        scratch_shapes=[pltpu.VMEM((2, 512, 1024), F32), dma((10,))],
+        scratch_shapes=[pltpu.VMEM((2, 512, 1024), F32), dma((26,))],
         compiler_params=pltpu.CompilerParams(vmem_limit_bytes=16 << 20),
         cost_estimate=pl.CostEstimate(flops=2 << 30, bytes_accessed=4 << 20, transcendentals=0),
     )(*(pltpu.with_memory_space_constraint(value, pltpu.VMEM) for value in held))

time: 40.1 us -> 39.4 us (0.983)
  Pallas kernels: 39.3 us -> 38.6 us
    pallas_call x1, Pallas kernels: 3.19 us -> 2.52 us  [body(): pl.pallas_call(write_kernel, out_shape=(jax.ShapeDtypeStruct((2, 32, 64),...]
where the time goes in v4:
time: 39.4 us; the launch traced here: 39.2 us
  Pallas kernels  38.6 us (98%)
  between operations  0.64 us (2%)
    pallas_call x1, Pallas kernels, body(): pl.pallas_call(gather_kernel, out_shape=(pltpu.VMEM((2, 32, 64), F32), pl...  36.1 us
    pallas_call x1, Pallas kernels, body(): pl.pallas_call(write_kernel, out_shape=(jax.ShapeDtypeStruct((2, 32, 64),...  2.52 us

profile of v4, /device:TPU:1, one launch (start us, length us, event | category | flops | bytes accessed | tf_op | source)
XLA Modules:
  0.0 39.2 jit_solution(477451005999162592)
XLA Ops:
  0.6 36.1 %shard_map.85 = (f32[2,32,64]{2,1,0:T(8,128)S(1)}, f32[2,32,64]{2,1,0:T(8,128)S(1)}, f32[2,512,1024]{2,1,0:T(8,128)S(1)}, bf16[2,2,512,1024]{3,2,1,0:T(8,128)(2,1)S(1)}, bf16[2,2,8,4,4,32,128]{6,5,4,3,2,1,0:T(8,128)(2,1)S(1)}) custom-call(f32[128,512]{1,0:T(8,128)} %bitcast.10, f32[128,512]{1,0:T(8,128)} %bitcast.11, f32[128,512]{1,0:T(8,128)} %bitcast.12, ...), custom_call_target="tpu_custom_call" | custom-call | flops 2147483648 | bytes 8388608 | tf_op jit(solution)/shard_map/pallas_call | solution.py:411
  36.7 2.5 %shard_map.86 = (f32[2,32,64]{2,1,0:T(8,128)}, f32[2,32,64]{2,1,0:T(8,128)}, f32[2,512,1024]{2,1,0:T(8,128)}) custom-call(f32[2,32,64]{2,1,0:T(8,128)S(1)} %get-tuple-element.11.first, f32[2,32,64]{2,1,0:T(8,128)S(1)} %get-tuple-element.12.second, f32[2,512,1024]{2,1,0:T(8,128)S(1)} %get-tuple-element.13.acc, ...), custom_call_target="tpu_custom_call" | custom-call | flops 2147483648 | bytes 4194304 | tf_op jit(solution)/shard_map/pallas_call | solution.py:454

commit v5 on v4

--- a/solution.py
+++ b/solution.py
@@ -298,6 +298,19 @@
     stage(net.open, 0)
 
     loads[4].wait()
+    loads[3].wait()
+    inv2_split[0], inv2_split[1] = split(inv2[...])
+
+    all_seven(sums, 0).wait_recv()
+    total = parts[rows]
+    for j in range(1, 2 * NX):
+        total += sums[j]
+    whole[rows] = head[pl.ds(pl.multiple_of(8 * rows, 8), 8), 512:] - total
+    for j in order:
+        share_copy(j).start()
+
+    stage(net.spread_plane, 0)
+    stage(net.spread_z, 0)
     for half in range(2):
         for at in range(NX):
             base = 512 * half + 128 * at
@@ -316,19 +329,6 @@
                 lhs[half, 0, :, k : k + 128] = plane0.astype(BF16)
                 lhs[half, 1, :, k : k + 128] = plane1.astype(BF16)
 
-    loads[3].wait()
-    inv2_split[0], inv2_split[1] = split(inv2[...])
-
-    all_seven(sums, 0).wait_recv()
-    total = parts[rows]
-    for j in range(1, 2 * NX):
-        total += sums[j]
-    whole[rows] = head[pl.ds(pl.multiple_of(8 * rows, 8), 8), 512:] - total
-    for j in order:
-        share_copy(j).start()
-
-    stage(net.spread_plane, 0)
-    stage(net.spread_z, 0)
     all_seven(whole, 2).wait_recv()
     solved = solve(whole[...].reshape(64, 512), (inv2_split[0], inv2_split[1]))
     gathered[1, core, 0, net.y, x] = solved.astype(BF16)
@@ -340,8 +340,8 @@
         update(acc, acc, lhs, gathered, half, steps, columns_of(net.z, steps), *one)
 
     stage(net.relay, 0)
+    stage(net.spread_z, 1)
     stage(net.spread_plane, 1)
-    stage(net.spread_z, 1)
     stage(net.take_slabs, 0)
     stage(net.take_far, 0, 0)
     stage(net.take_far, 0, 1)

time: 39.4 us -> 38.6 us (0.980)
  Pallas kernels: 38.6 us -> 37.9 us
    pallas_call x1, Pallas kernels: 36.1 us -> 35.3 us  [body(): pl.pallas_call(gather_kernel, out_shape=(pltpu.VMEM((2, 32, 64), F32), pl...]
where the time goes in v5:
time: 38.6 us; the launch traced here: 38.5 us
  Pallas kernels  37.9 us (98%)
  between operations  0.64 us (2%)
    pallas_call x1, Pallas kernels, body(): pl.pallas_call(gather_kernel, out_shape=(pltpu.VMEM((2, 32, 64), F32), pl...  35.3 us
    pallas_call x1, Pallas kernels, body(): pl.pallas_call(write_kernel, out_shape=(jax.ShapeDtypeStruct((2, 32, 64),...  2.52 us

profile of v5, /device:TPU:1, one launch (start us, length us, event | category | flops | bytes accessed | tf_op | source)
XLA Modules:
  0.0 38.5 jit_solution(10876538323606652545)
XLA Ops:
  0.6 35.3 %shard_map.85 = (f32[2,32,64]{2,1,0:T(8,128)S(1)}, f32[2,32,64]{2,1,0:T(8,128)S(1)}, f32[2,512,1024]{2,1,0:T(8,128)S(1)}, bf16[2,2,512,1024]{3,2,1,0:T(8,128)(2,1)S(1)}, bf16[2,2,8,4,4,32,128]{6,5,4,3,2,1,0:T(8,128)(2,1)S(1)}) custom-call(f32[128,512]{1,0:T(8,128)} %bitcast.10, f32[128,512]{1,0:T(8,128)} %bitcast.11, f32[128,512]{1,0:T(8,128)} %bitcast.12, ...), custom_call_target="tpu_custom_call" | custom-call | flops 2147483648 | bytes 8388608 | tf_op jit(solution)/shard_map/pallas_call | solution.py:411
  36.0 2.5 %shard_map.86 = (f32[2,32,64]{2,1,0:T(8,128)}, f32[2,32,64]{2,1,0:T(8,128)}, f32[2,512,1024]{2,1,0:T(8,128)}) custom-call(f32[2,32,64]{2,1,0:T(8,128)S(1)} %get-tuple-element.11.first, f32[2,32,64]{2,1,0:T(8,128)S(1)} %get-tuple-element.12.second, f32[2,512,1024]{2,1,0:T(8,128)S(1)} %get-tuple-element.13.acc, ...), custom_call_target="tpu_custom_call" | custom-call | flops 2147483648 | bytes 4194304 | tf_op jit(solution)/shard_map/pallas_call | solution.py:454

commit v6 on v5

--- a/solution.py
+++ b/solution.py
@@ -144,6 +144,12 @@
         self.wait(half, (NZ - 1 - 2 * near, 1, 1), landed=ALONG_Z)
         for i, j in [(2, 2), (1, 2), (3, 2), (0, 2), (2, 1), (1, 1), (3, 1), (0, 1), (2, 3), (1, 3), (3, 3), (0, 3), (2, 0), (1, 0), (3, 0)]:
             self.far_over(half, near, i, j).start()
+
+    def take_slab(self, half, near, step):
+        if step <= near:
+            self.wait(half, (2, NY, NX), landed=SLABS + step)
+            for dz in (step, NZ - step):
+                self.hand_on(half, self.slab(half, dz), NEAR_ON if step == 1 else SLABS_ON)
 
     def take_slabs(self, half, near):
         for step in range(2 if half in RELAY else 1, near + 1):
@@ -358,10 +364,11 @@
     product(0, (7, 2))
     product(0, (6, 3))
     product(0, (5, 4))
-    stage(net.take_slabs, 1)
+    stage(net.take_slab, 1, 1)
     stage(net.take_far, 1, 0)
     stage(net.take_far, 1, 1)
     stage(net.take_far, 1, 3)
+    stage(net.take_slab, 1, 2)
     stage(net.take_far, 1, 2)
     net.finish_near(1)
     product(1, (0, 1))

time: 38.6 us -> 38.3 us (level)
  no operation moved by 1% of the time
where the time goes in v6:
time: 38.3 us; the launch traced here: 38.2 us
  Pallas kernels  37.6 us (98%)
  between operations  0.64 us (2%)
    pallas_call x1, Pallas kernels, body(): pl.pallas_call(gather_kernel, out_shape=(pltpu.VMEM((2, 32, 64), F32), pl...  35.1 us
    pallas_call x1, Pallas kernels, body(): pl.pallas_call(write_kernel, out_shape=(jax.ShapeDtypeStruct((2, 32, 64),...  2.53 us

profile of v6, /device:TPU:1, one launch (start us, length us, event | category | flops | bytes accessed | tf_op | source)
XLA Modules:
  0.0 38.2 jit_solution(4731792817107291960)
XLA Ops:
  0.6 35.1 %shard_map.85 = (f32[2,32,64]{2,1,0:T(8,128)S(1)}, f32[2,32,64]{2,1,0:T(8,128)S(1)}, f32[2,512,1024]{2,1,0:T(8,128)S(1)}, bf16[2,2,512,1024]{3,2,1,0:T(8,128)(2,1)S(1)}, bf16[2,2,8,4,4,32,128]{6,5,4,3,2,1,0:T(8,128)(2,1)S(1)}) custom-call(f32[128,512]{1,0:T(8,128)} %bitcast.10, f32[128,512]{1,0:T(8,128)} %bitcast.11, f32[128,512]{1,0:T(8,128)} %bitcast.12, ...), custom_call_target="tpu_custom_call" | custom-call | flops 2147483648 | bytes 8388608 | tf_op jit(solution)/shard_map/pallas_call | solution.py:418
  35.7 2.5 %shard_map.86 = (f32[2,32,64]{2,1,0:T(8,128)}, f32[2,32,64]{2,1,0:T(8,128)}, f32[2,512,1024]{2,1,0:T(8,128)}) custom-call(f32[2,32,64]{2,1,0:T(8,128)S(1)} %get-tuple-element.11.first, f32[2,32,64]{2,1,0:T(8,128)S(1)} %get-tuple-element.12.second, f32[2,512,1024]{2,1,0:T(8,128)S(1)} %get-tuple-element.13.acc, ...), custom_call_target="tpu_custom_call" | custom-call | flops 2147483648 | bytes 4194304 | tf_op jit(solution)/shard_map/pallas_call | solution.py:461
